TPU v7x, 128 devices: a whole 4x4x4 slice. The times are simulated.
128 devices in a mesh: ctx: 8 (over z, y_hi), exp: 16 (over x, y_lo, core).
Axes of the slice: x: 4, y: 4 (y_hi: 2, y_lo: 2; y = y_hi * 2 + y_lo), z: 4, core: 2. Of those that a mesh axis runs over, the one named last changes fastest.
Arguments:
- q_nope: bfloat16 [2048, 16384], P('ctx', 'exp'), may hold values from -6 to 6
- q_rope: bfloat16 [2048, 8192], P('ctx', 'exp'), may hold values from -24 to 24
- kv_latent: bfloat16 [2048, 512], P('ctx'), may hold values from -6 to 6
- key_rope: bfloat16 [2048, 64], P('ctx'), may hold values from -6 to 6
- w_uk: bfloat16 [128, 128, 512], P('exp'), may hold values from -0.5 to 0.5
- w_uv: bfloat16 [128, 512, 128], P('exp'), may hold values from -1 to 1
- w_out: bfloat16 [16384, 7168], P('exp', 'ctx'), may hold values from -0.09375 to 0.09375
- w_gate: bfloat16 [16, 7168, 2048], P('exp', 'ctx'), may hold values from -0.0625 to 0.0625
- w_up: bfloat16 [16, 7168, 2048], P('exp', 'ctx'), may hold values from -0.0625 to 0.0625
- w_down: bfloat16 [16, 2048, 7168], P('exp', None, 'ctx'), may hold values from -0.125 to 0.125
- route_ids: int32 [2048, 4], P('exp'), may hold values from 0 to 15, all different within a row; in each aligned block of 128 rows (0 to 127, 128 to 255, ...) at most 48 rows name the same one
- route_gates: bfloat16 [2048, 4], P('exp'), may hold values from 0.19921875 to 1
Outputs:
- attn_out: bfloat16 [2048, 7168], P('exp', 'ctx')
- moe_out: bfloat16 [2048, 7168], P('exp', 'ctx')
Inputs may be any that keep to these rules, and one draw needn't show every extreme that they name: `route_ids`: each row names 4 different experts. In each aligned block of 128 rows no expert is named by more than 48 rows, and in some block one expert is named by exactly 48 rows.
All inputs are finite; a program needn't handle non-finite values.
Results may differ from a plain program's by a relative error of at most 0.035.
Values may be sent and summed in bfloat16 or wider, within the bound.
No kernel may reach another device: no remote copies, remote signals or barrier semaphores. Data moves between devices by JAX's collectives and lax.ppermute only.
A program may use at most 128 MiB of HBM per device.

v0:
```python
import functools
import math

import jax
import jax.numpy as jnp
from jax import lax
from jax.experimental import pallas as pl
from jax.experimental.pallas import tpu as pltpu
from jax.sharding import PartitionSpec as P

BF = jnp.bfloat16
F32 = jnp.float32
NEG_FILL = -1e30
PIECE = 128

ZS = 4
AG_ORDER = ((0, 0), (-1, 0), (1, 0), (0, 1), (-1, 1), (1, 1), (2, 0), (2, 1))


def z_shift(array, step):
    perm = [(z * 2 + y, ((z + step) % ZS) * 2 + y) for z in range(ZS) for y in range(2)]
    return lax.ppermute(array, "ctx", perm)


def y_swap(array):
    return lax.ppermute(array, "ctx", [(i, i ^ 1) for i in range(2 * ZS)])


def x_shift(array, step):
    perm = [(x * 4 + r, ((x + step) % 4) * 4 + r) for x in range(4) for r in range(4)]
    return lax.ppermute(array, "exp", perm)


def near_swap(array):
    return lax.ppermute(array, "exp", [(e, e ^ 2) for e in range(16)])


def core_swap(array):
    return lax.ppermute(array, "exp", [(e, e ^ 1) for e in range(16)])


def ctx_at(here, dz, dy):
    z, y = here // 2, here % 2
    return ((z + dz) % ZS) * 2 + (y + dy) % 2


def first_blocks(own):
    return own, z_shift(own, 1), z_shift(own, -1), y_swap(own)


def gather_blocks(own):
    return other_blocks(first_blocks(own))


def other_blocks(blocks):
    own, up, down, side = blocks
    half = own.shape[0] // 2
    far = jnp.concatenate([z_shift(up[:half], 1), z_shift(down[half:], -1)], axis=0)
    side_up, side_down = z_shift(side, 1), z_shift(side, -1)
    return own, up, down, side, side_up, side_down, far, y_swap(far)


def add(*terms):
    return functools.reduce(jnp.add, [t.astype(F32) for t in terms])


def scatter_sum(part, shift, swap):
    got_far = swap(part(2, 1))
    got_up, got_down = shift(part(1, 1), 1), shift(part(-1, 1), -1)
    far = add(part(2, 0), got_far).astype(BF)
    half = far.shape[0] // 2
    far_up, far_down = shift(far[:half], 1), shift(far[half:], -1)
    got_side = swap(add(part(0, 1), got_up, got_down).astype(BF))
    up, down = part(1, 0), part(-1, 0)
    up = jnp.concatenate([add(up[:half], far_up).astype(BF), up[half:]], axis=0)
    down = jnp.concatenate([down[:half], add(down[half:], far_down).astype(BF)], axis=0)
    return add(part(0, 0), got_side, shift(up, 1), shift(down, -1))


def attention_kernel(where_ref, qn_ref, qr_ref, uk_ref, uv_ref, *refs, scale):
    *piece_refs, mine_ref, other_ref, keys = refs
    rows = qn_ref.shape[0]
    even = where_ref[keys.shape[0] // PIECE] == 0
    heads, nope, latent = uk_ref.shape
    vhead = uv_ref.shape[2]
    rope = qr_ref.shape[1] // heads
    factor = scale * math.log2(math.e)

    @pl.when(pl.program_id(0) == 0)
    def _():
        at = 0
        for ref in piece_refs:
            keys[at : at + ref.shape[0], :] = ref[...]
            at += ref.shape[0]

    lanes = lax.broadcasted_iota(jnp.int32, (rows, 2 * rope), 1)
    ahead = lax.broadcasted_iota(jnp.int32, (rows, PIECE), 0) - lax.broadcasted_iota(
        jnp.int32, (rows, PIECE), 1
    )

    def score(h):
        plain = jnp.dot(
            qn_ref[:, h * nope : (h + 1) * nope], uk_ref[h], preferred_element_type=F32
        ).astype(BF)
        first = h // 2 * 2 * rope
        mine = (lanes >= h % 2 * rope) & (lanes < (h % 2 + 1) * rope)
        turned = jnp.where(mine, qr_ref[:, first : first + 2 * rope], jnp.zeros((), BF))
        scores = lax.dot_general(
            jnp.concatenate([plain, turned], axis=1),
            keys[...],
            (((1,), (1,)), ((), ())),
            preferred_element_type=F32,
        )
        return jnp.concatenate(
            [
                jnp.where(ahead >= where_ref[p], scores[:, p * PIECE : (p + 1) * PIECE], NEG_FILL)
                for p in range(keys.shape[0] // PIECE)
            ],
            axis=1,
        )

    later = score(0)
    for h in range(heads):
        scores, later = later, score(h + 1) if h + 1 < heads else None
        largest = jnp.max(scores, axis=1, keepdims=True)
        terms = jnp.exp2((scores - largest) * factor)
        total = jnp.sum(terms, axis=1, keepdims=True)
        mixed = jnp.dot(terms.astype(BF), keys[:, :latent], preferred_element_type=F32)
        mixed = (mixed / total).astype(BF)
        head = jnp.dot(mixed, uv_ref[h], preferred_element_type=F32).astype(BF)
        low, high = head[: rows // 2], head[rows // 2 :]
        mine_ref[:, h * vhead : (h + 1) * vhead] = jnp.where(even, low, high)
        other_ref[:, h * vhead : (h + 1) * vhead] = jnp.where(even, high, low)


def attention(where, core, q_nope, q_rope, pieces, w_uk, w_uv):
    rows = q_nope.shape[0]
    heads, nope, latent = w_uk.shape
    vhead = w_uv.shape[2]
    rope = q_rope.shape[1] // heads
    group = 4
    key_count = sum(p.shape[0] for p in pieces)
    width = pieces[0].shape[1]
    return pl.pallas_call(
        functools.partial(attention_kernel, scale=1.0 / math.sqrt(nope + rope)),
        grid_spec=pltpu.PrefetchScalarGridSpec(
            num_scalar_prefetch=1,
            grid=(heads // group,),
            in_specs=[
                pl.BlockSpec((rows, group * nope), lambda i, w: (0, i)),
                pl.BlockSpec((rows, group * rope), lambda i, w: (0, i)),
                pl.BlockSpec((group, nope, latent), lambda i, w: (i, 0, 0)),
                pl.BlockSpec((group, latent, vhead), lambda i, w: (i, 0, 0)),
            ]
            + [pl.BlockSpec(p.shape, lambda i, w: (0, 0)) for p in pieces],
            out_specs=[pl.BlockSpec((rows // 2, group * vhead), lambda i, w: (0, i))] * 2,
            scratch_shapes=[pltpu.VMEM((key_count, width), BF)],
        ),
        out_shape=[jax.ShapeDtypeStruct((rows // 2, heads * vhead), BF)] * 2,
        compiler_params=pltpu.CompilerParams(vmem_limit_bytes=60 * 2**20),
        cost_estimate=pl.CostEstimate(
            flops=2 * rows * heads * key_count * (width + latent),
            bytes_accessed=2 * (key_count * width + 2 * q_nope.size),
            transcendentals=rows * heads * key_count,
        ),
    )(jnp.append(where, core), q_nope, q_rope, w_uk, w_uv, *pieces)


def project_kernel(places_ref, *refs, depths, count, before):
    weight_refs, refs = refs[: len(depths)], refs[len(depths) :]
    block_refs, refs = refs[:count], refs[count:]
    *before_refs, out_ref, weights, blocks, sem = refs
    rows = block_refs[0].shape[0]
    copies, at = [], 0
    for ref, depth in zip(weight_refs, depths, strict=True):
        copies.append((ref, weights.at[pl.ds(at, depth)]))
        at += depth
    for n, ref in enumerate(block_refs):
        copies.append((ref, blocks.at[pl.ds(n * rows, rows)]))
    copies = [pltpu.make_async_copy(a, b, sem.at[n]) for n, (a, b) in enumerate(copies)]
    for copy in copies:
        copy.start()
    for ref in before_refs:
        for b in range(before):
            out_ref[places_ref[b]] = ref[b]
    for copy in copies:
        copy.wait()
    result = jnp.dot(blocks[...], weights[...], preferred_element_type=F32).astype(BF)
    for b in range(count):
        slot = places_ref[before + b] if before_refs else b
        out_ref[slot] = result[b * rows : (b + 1) * rows]


def project(weights, blocks, places, earlier=None):
    rows = blocks[0].shape[0]
    columns = weights[0].shape[1]
    depths = [w.shape[0] for w in weights]
    before = 0 if earlier is None else earlier.shape[0]
    vmem = pl.BlockSpec(memory_space=pltpu.VMEM)
    kernel = functools.partial(project_kernel, depths=depths, count=len(blocks), before=before)
    return pl.pallas_call(
        kernel,
        in_specs=[pl.BlockSpec(memory_space=pltpu.SMEM)]
        + [pl.BlockSpec(memory_space=pl.ANY)] * (len(weights) + len(blocks))
        + [vmem] * (before > 0),
        out_specs=vmem,
        out_shape=jax.ShapeDtypeStruct((before + len(blocks), rows, columns), BF),
        scratch_shapes=[
            pltpu.VMEM((sum(depths), columns), BF),
            pltpu.VMEM((len(blocks) * rows, sum(depths)), BF),
            pltpu.SemaphoreType.DMA((len(weights) + len(blocks),)),
        ],
        compiler_params=pltpu.CompilerParams(vmem_limit_bytes=40 * 2**20),
        cost_estimate=pl.CostEstimate(
            flops=2 * len(blocks) * rows * sum(depths) * columns,
            bytes_accessed=2 * (sum(depths) * columns + len(blocks) * rows * (sum(depths) + columns)),
            transcendentals=0,
        ),
    )(places, *weights, *blocks, *([] if earlier is None else [earlier]))


def combine_kernel(order_ref, w_ref, *refs, count):
    block_refs, refs = refs[:count], refs[count:]
    *before_refs, out_ref, weights, blocks, sem = refs
    step = block_refs[0].shape[1]
    copies = []
    for n, ref in enumerate(block_refs):
        start = pl.multiple_of(order_ref[n] * step, step)
        source = w_ref.at[0, pl.ds(start, step)]
        copies.append((source, weights.at[pl.ds(n * step, step)]))
        copies.append((ref, blocks.at[:, pl.ds(n * step, step)]))
    copies = [pltpu.make_async_copy(a, b, sem.at[n]) for n, (a, b) in enumerate(copies)]
    for copy in copies:
        copy.start()
    for copy in copies:
        copy.wait()
    result = jnp.dot(blocks[...], weights[...], preferred_element_type=F32)
    for ref in before_refs:
        result = result + ref[...]
    out_ref[...] = result.astype(out_ref.dtype)


def combine(order, w_down, blocks, dtype, earlier=()):
    rows, step = blocks[0].shape
    columns = w_down.shape[2]
    depth = len(blocks) * step
    vmem = pl.BlockSpec(memory_space=pltpu.VMEM)
    return pl.pallas_call(
        functools.partial(combine_kernel, count=len(blocks)),
        in_specs=[pl.BlockSpec(memory_space=pltpu.SMEM)]
        + [pl.BlockSpec(memory_space=pl.ANY)] * (1 + len(blocks))
        + [vmem] * len(earlier),
        out_specs=vmem,
        out_shape=jax.ShapeDtypeStruct((rows, columns), dtype),
        scratch_shapes=[
            pltpu.VMEM((depth, columns), BF),
            pltpu.VMEM((rows, depth), BF),
            pltpu.SemaphoreType.DMA((2 * len(blocks),)),
        ],
        compiler_params=pltpu.CompilerParams(vmem_limit_bytes=40 * 2**20),
        cost_estimate=pl.CostEstimate(
            flops=2 * rows * depth * columns,
            bytes_accessed=2 * (depth * columns + rows * depth + 2 * rows * columns),
            transcendentals=0,
        ),
    )(jnp.stack(order), w_down, *blocks, *earlier)


def local(
    q_nope,
    q_rope,
    kv_latent,
    key_rope,
    w_uk,
    w_uv,
    w_out,
    w_gate,
    w_up,
    w_down,
    route_ids,
    route_gates,
):
    tok_rows = q_nope.shape[0]
    ctx_here = lax.axis_index("ctx")
    core = lax.axis_index("exp") % 2
    ctx_size = lax.axis_size("ctx")
    order = [ctx_at(ctx_here, dz, dy) for dz, dy in AG_ORDER]

    key_rows = jnp.concatenate([kv_latent, key_rope, key_rope], axis=1)
    half_rows = tok_rows // 2
    blocks = gather_blocks(lax.dynamic_slice_in_dim(key_rows, core * half_rows, half_rows, 0))
    pieces, starts = [key_rows], [ctx_here * tok_rows, ctx_here * tok_rows + half_rows]
    for block, source in zip(blocks[1:], order[1:], strict=True):
        pieces += [block, core_swap(block)]
        starts += [
            source * tok_rows + core * half_rows,
            source * tok_rows + (1 - core) * half_rows,
        ]
    where = jnp.stack(starts) - ctx_here * tok_rows

    mine, other = attention(where, core, q_nope, q_rope, pieces, w_uk, w_uv)

    blocks = gather_blocks(jnp.concatenate([mine, core_swap(other)], axis=1))
    weights = [w_out, core_swap(w_out)]
    first, last = [0, 1, 2, 3, 6], [4, 5, 7]
    chip = lax.axis_index("exp") // 2
    slots = jnp.stack(
        [((order[b] // 2 - chip // 2) % 4) * 2 + (order[b] + chip) % 2 for b in first + last]
    )
    early = project(weights, [blocks[b] for b in first], slots)
    pair_sum = project(weights, [blocks[b] for b in last], slots, early)
    attn_out = scatter_sum(
        lambda step, side: pair_sum[(step % 4) * 2 + side], x_shift, near_swap
    ).astype(BF)

    out_rows = attn_out.shape[0]
    feature_cols = attn_out.shape[1]
    top_count = route_ids.shape[1]
    expert_count = lax.axis_size("exp") * w_gate.shape[0]
    capacity = 3 * out_rows * top_count // (2 * expert_count)
    slot_total = expert_count * capacity
    flat_ids = route_ids.reshape(-1)
    onehot = (flat_ids[:, None] == jnp.arange(expert_count, dtype=jnp.int32)[None, :]).astype(
        jnp.int32
    )
    earlier = jnp.cumsum(onehot, axis=0) - onehot
    slot_ids = jnp.sum(earlier * onehot, axis=1)
    targets = (flat_ids * capacity + slot_ids).reshape(out_rows, top_count)
    slot_range = jnp.arange(slot_total, dtype=jnp.int32)
    hits = targets[:, :, None] == slot_range[None, None, :]
    placing = jnp.sum(hits.astype(F32), axis=1).astype(BF).T
    weighting = jnp.sum(jnp.where(hits, route_gates[:, :, None], jnp.zeros((), BF)), axis=1)
    send_rows = jnp.dot(placing, attn_out, preferred_element_type=F32).astype(BF)
    send_rows = send_rows.reshape(expert_count, capacity, feature_cols)
    arrived = lax.all_to_all(send_rows, "exp", split_axis=0, concat_axis=0, tiled=True)
    flat_rows = arrived.reshape(slot_total, feature_cols)

    hidden_cols = w_gate.shape[2] // ctx_size

    def part(dz, dy):
        first = ctx_at(ctx_here, dz, dy) * hidden_cols
        both = jnp.concatenate(
            [lax.dynamic_slice_in_dim(w[0], first, hidden_cols, 1) for w in (w_gate, w_up)], axis=1
        )
        return jnp.dot(flat_rows, both, preferred_element_type=F32).astype(BF)

    pre = scatter_sum(part, z_shift, y_swap)
    hidden = (jax.nn.silu(pre[:, :hidden_cols]) * pre[:, hidden_cols:]).astype(BF)
    all_hidden = gather_blocks(hidden)
    early = combine([order[b] for b in first], w_down, [all_hidden[b] for b in first], F32)
    expert_out = combine([order[b] for b in last], w_down, [all_hidden[b] for b in last], BF, [early])
    expert_out = expert_out.reshape(expert_count, capacity, feature_cols)
    returned = lax.all_to_all(expert_out, "exp", split_axis=0, concat_axis=0, tiled=True)
    moe_out = jnp.dot(
        weighting, returned.reshape(slot_total, feature_cols), preferred_element_type=F32
    ).astype(BF)
    return (attn_out, moe_out)


def solution(mesh):
    placed = (
        P("ctx", "exp"),
        P("ctx", "exp"),
        P("ctx", None),
        P("ctx", None),
        P("exp", None, None),
        P("exp", None, None),
        P("exp", "ctx"),
        P("exp", "ctx", None),
        P("exp", "ctx", None),
        P("exp", None, "ctx"),
        P("exp", None),
        P("exp", None),
    )
    return jax.shard_map(
        local,
        mesh=mesh,
        in_specs=placed,
        out_specs=(P("exp", "ctx"), P("exp", "ctx")),
        check_vma=False,
    )
```

profile of v0, /device:TPU:1, one launch (start us, length us, event | category | flops | bytes accessed | tf_op | source)
XLA Modules:
  0.0 259.5 jit_solution(18088544749427472123)
XLA Ops:
  1.5 1.0 pad_maximum_fusion.2.refs_0_
  2.6 2.5 collective-permute-start.1
  5.2 2.2 collective-permute-start.3
  7.4 2.9 %collective-permute-start.5 = (bf16[128,640]{1,0:T(8,128)(2,1)S(1)}, bf16[128,640]{1,0:T(8,128)(2,1)S(1)}, u32[]{:S(2)}, u32[]{:S(2)}) collective-permute-start(bf16[128,640]{1,0:T(8,128)(2,1)S(1)} %constant_dynamic-slice_fusion), channel_id=1, source_target_pairs={{0,16},{16,0},{32,48},{48,32},{64,80},{80,64},{96,112},{112,96},{1... | collective-permute-start | bytes 491528 | tf_op jit(solution)/shard_map/ppermute | solution.py:26
  11.3 2.7 %collective-permute-start.12 = (bf16[64,640]{1,0:T(8,128)(2,1)S(1)}, bf16[64,640]{1,0:T(8,128)(2,1)S(1)}, u32[]{:S(2)}, u32[]{:S(2)}) collective-permute-start(bf16[64,640]{1,0:T(8,128)(2,1)S(1)} %slice.129), channel_id=1, source_target_pairs={{0,96},{16,112},{32,0},{48,16},{64,32},{80,48},{96,64},{112,80},{1... | collective-permute-start | bytes 245768 | tf_op jit(solution)/shard_map/ppermute | solution.py:22
  14.4 1.1 collective-permute-start.7
  15.5 2.3 collective-permute-start.6
  18.2 3.0 %collective-permute-start.14 = (bf16[128,640]{1,0:T(8,128)(2,1)S(1)}, bf16[128,640]{1,0:T(8,128)(2,1)}, u32[]{:S(2)}, u32[]{:S(2)}) collective-permute-start(bf16[128,640]{1,0:T(8,128)(2,1)S(1)} %constant_dynamic-update-slice_fusion.refs_11_), channel_id=1, source_target_pairs={{0,16},{16,0},{32,48},{48,32},{64,80},{80,64},{96,112},{112,96},{1... | collective-permute-start | bytes 491528 | tf_op jit(solution)/shard_map/ppermute | solution.py:26
  22.0 1.7 collective-permute-start.13
  24.2 1.2 collective-permute-done.14.refs_13_
  25.4 1.2 collective-permute-start.15
  28.2 19.5 %shard_map.131 = (bf16[128,1024]{1,0:T(8,128)(2,1)}, bf16[128,1024]{1,0:T(8,128)(2,1)}) custom-call(s32[17]{0:T(128)} %pad_add_fusion.where_ref, bf16[256,1024]{1,0:T(8,128)(2,1)} %qn_ref.1, bf16[256,512]{1,0:T(8,128)(2,1)} %qr_ref.1, bf16[8,128,512]{2,1,0:T(8,128)(2,1)} %uk_ref.1, bf16[8,512,128]{2,1,0:T(8,128)(2,1)} %uv_ref.1, ...), custom_call_target="tpu_custom_call" | custom-call | flops 9663676416 | bytes 3670016 | tf_op jit(solution)/shard_map/pallas_call | solution.py:144
  49.6 2.7 %collective-permute-start.22 = (bf16[128,2048]{1,0:T(8,128)(2,1)S(1)}, bf16[128,2048]{1,0:T(8,128)(2,1)S(1)}, u32[]{:S(2)}, u32[]{:S(2)}) collective-permute-start(bf16[128,2048]{1,0:T(8,128)(2,1)S(1)} %constant_dynamic-update-slice_fusion.2.refs_2_), channel_id=1, source_target_pairs={{0,96},{16,112},{32,0},{48,16},{64,32},{80,48},{96,64},{112,80},{1... | collective-permute-start | bytes 1572872 | tf_op jit(solution)/shard_map/ppermute | solution.py:22
  52.3 2.9 %collective-permute-start.17 = (bf16[128,2048]{1,0:T(8,128)(2,1)S(1)}, bf16[128,2048]{1,0:T(8,128)(2,1)}, u32[]{:S(2)}, u32[]{:S(2)}) collective-permute-start(bf16[128,2048]{1,0:T(8,128)(2,1)S(1)} %constant_dynamic-update-slice_fusion.2.refs_2_), channel_id=1, source_target_pairs={{0,16},{16,0},{32,48},{48,32},{64,80},{80,64},{96,112},{112,96},{1... | collective-permute-start | bytes 1572872 | tf_op jit(solution)/shard_map/ppermute | solution.py:26
  55.2 8.9 %collective-permute-done.20.refs_3_ = bf16[128,2048]{1,0:T(8,128)(2,1)S(1)} collective-permute-done((bf16[128,2048]{1,0:T(8,128)(2,1)S(1)}, bf16[128,2048]{1,0:T(8,128)(2,1)S(1)}, u32[]{:S(2)}, u32[]{:S(2)}) %collective-permute-start.20) | collective-permute-done | bytes 524320 | tf_op jit(solution)/shard_map/ppermute | solution.py:22
  64.2 2.7 %collective-permute-start.23 = (bf16[64,2048]{1,0:T(8,128)(2,1)S(1)}, bf16[64,2048]{1,0:T(8,128)(2,1)S(1)}, u32[]{:S(2)}, u32[]{:S(2)}) collective-permute-start(bf16[64,2048]{1,0:T(8,128)(2,1)S(1)} %slice.131), channel_id=1, source_target_pairs={{0,96},{16,112},{32,0},{48,16},{64,32},{80,48},{96,64},{112,80},{1... | collective-permute-start | bytes 786440 | tf_op jit(solution)/shard_map/ppermute | solution.py:22
  66.9 2.7 %collective-permute-start.19 = (bf16[128,2048]{1,0:T(8,128)(2,1)}, bf16[128,2048]{1,0:T(8,128)(2,1)S(1)}, u32[]{:S(2)}, u32[]{:S(2)}) collective-permute-start(bf16[128,2048]{1,0:T(8,128)(2,1)} %collective-permute-done.17.refs_5_), channel_id=1, source_target_pairs={{0,96},{16,112},{32,0},{48,16},{64,32},{80,48},{96,64},{112,80},{1... | collective-permute-start | bytes 1572872 | tf_op jit(solution)/shard_map/ppermute | solution.py:22
  69.6 2.5 collective-permute-done.21
  73.5 3.0 %collective-permute-start.24 = (bf16[128,2048]{1,0:T(8,128)(2,1)}, bf16[128,2048]{1,0:T(8,128)(2,1)S(1)}, u32[]{:S(2)}, u32[]{:S(2)}) collective-permute-start(bf16[128,2048]{1,0:T(8,128)(2,1)} %constant_dynamic-update-slice_fusion.4.refs_6_), channel_id=1, source_target_pairs={{0,16},{16,0},{32,48},{48,32},{64,80},{80,64},{96,112},{112,96},{1... | collective-permute-start | bytes 1572872 | tf_op jit(solution)/shard_map/ppermute | solution.py:26
  77.0 1.2 copy-done.5
  78.1 1.0 copy-done.7
  79.2 1.0 copy-done.9
  80.2 5.4 %shard_map.132.refs_5_ = bf16[5,128,896]{2,1,0:T(8,128)(2,1)S(1)} custom-call(s32[8]{0:T(128)S(1)} %stack.116.places_ref, bf16[1024,896]{1,0:T(8,128)(2,1)S(1)} %copy-done.2, bf16[1024,896]{1,0:T(8,128)(2,1)} %collective-permute-done.refs_1_, bf16[128,2048]{1,0:T(8,128)(2,1)S(1)} %copy-done.9, bf16[128,2048]{1,0:T(8,128)(2,1)S(1)} %copy-done.5, ...), custom_call_target="tpu_custom_call" | custom-call | flops 2348810240 | bytes 7438336 | tf_op jit(solution)/shard_map/pallas_call | solution.py:201
  85.6 4.0 %shard_map.133 = bf16[8,128,896]{2,1,0:T(8,128)(2,1)S(1)} custom-call(s32[8]{0:T(128)S(1)} %stack.116.places_ref, bf16[1024,896]{1,0:T(8,128)(2,1)S(1)} %copy-done.3, bf16[1024,896]{1,0:T(8,128)(2,1)} %collective-permute-done.refs_1_, bf16[128,2048]{1,0:T(8,128)(2,1)S(1)} %collective-permute-done.18.refs_2_, ...), custom_call_target="tpu_custom_call" | custom-call | flops 1409286144 | bytes 5931008 | tf_op jit(solution)/shard_map/pallas_call | solution.py:201
  89.7 1.2 collective-permute-start.25
  90.9 1.6 collective-permute-start.26
  93.2 1.2 reduce-window.6
  94.8 1.0 collective-permute-done.25
  95.8 1.5 collective-permute-done.28
  97.6 2.7 %collective-permute-start.31 = (bf16[64,896]{1,0:T(8,128)(2,1)S(1)}, bf16[64,896]{1,0:T(8,128)(2,1)S(1)}, u32[]{:S(2)}, u32[]{:S(2)}) collective-permute-start(bf16[64,896]{1,0:T(8,128)(2,1)S(1)} %get-tuple-element.34), channel_id=1, source_target_pairs={{0,12},{1,13},{2,14},{3,15},{4,0},{5,1},{6,2},{7,3},{8,4},{9,5},{1... | collective-permute-start | bytes 344072 | tf_op jit(solution)/shard_map/ppermute | solution.py:31
  100.9 1.5 collective-permute-done.29
  102.5 1.2 collective-permute-start.30
  103.7 1.7 collective-permute-start.32
  105.6 4.4 %collective-permute-done.30 = bf16[128,896]{1,0:T(8,128)(2,1)S(1)} collective-permute-done((bf16[128,896]{1,0:T(8,128)(2,1)S(1)}, bf16[128,896]{1,0:T(8,128)(2,1)S(1)}, u32[]{:S(2)}, u32[]{:S(2)}) %collective-permute-start.30) | collective-permute-done | bytes 229408 | tf_op jit(solution)/shard_map/ppermute | solution.py:31
  110.2 1.7 convolution_convert_fusion
  111.8 13.3 %all-to-all-start = ((bf16[16,48,896]{2,1,0:T(8,128)(2,1)}), bf16[16,48,896]{2,1,0:T(8,128)(2,1)S(1)}, u32[]{:S(2)}, u32[]{:S(2)}) async-start(bf16[16,48,896]{2,1,0:T(8,128)(2,1)} %bitcast.39), calls=%async_computation | async-start | bytes 2752512 | tf_op jit(solution)/shard_map/all_to_all | solution.py:335
  125.1 5.6 %dynamic-slice_bitcast_fusion.14 = (bf16[896,256]{1,0:T(8,128)(2,1)S(1)}, bf16[896,256]{1,0:T(8,128)(2,1)}, bf16[896,256]{1,0:T(8,128)(2,1)}, bf16[896,256]{1,0:...) fusion(bf16[1,896,2048]{2,1,0:T(8,128)(2,1)} %param.20, ...), kind=kLoop, calls=%fused_computation.70 | loop fusion | bytes 14680096 | tf_op jit(solution)/shard_map/dynamic_slice | solution.py:343
  130.7 13.6 %all-to-all-done = bf16[16,48,896]{2,1,0:T(8,128)(2,1)S(1)} async-done(((bf16[16,48,896]{2,1,0:T(8,128)(2,1)}), bf16[16,48,896]{2,1,0:T(8,128)(2,1)S(1)}, u32[]{:S(2)}, u32[]{:S(2)}) %all-to-all-start) | async-done | bytes 1376288 | tf_op jit(solution)/shard_map/all_to_all | solution.py:335
  144.3 2.2 convolution_convert_fusion.2
  146.5 2.9 %collective-permute-start.36 = (bf16[768,512]{1,0:T(8,128)(2,1)S(1)}, bf16[768,512]{1,0:T(8,128)(2,1)S(1)}, u32[]{:S(2)}, u32[]{:S(2)}) collective-permute-start(bf16[768,512]{1,0:T(8,128)(2,1)S(1)} %convolution_convert_fusion.2), channel_id=1, source_target_pairs={{0,16},{16,0},{32,48},{48,32},{64,80},{80,64},{96,112},{112,96},{1... | collective-permute-start | bytes 2359304 | tf_op jit(solution)/shard_map/ppermute | solution.py:26
  149.5 1.0 convolution_convert_fusion.6
  150.7 1.0 convolution_convert_fusion.5
  151.6 2.9 %collective-permute-start.34 = (bf16[768,512]{1,0:T(8,128)(2,1)S(1)}, bf16[768,512]{1,0:T(8,128)(2,1)S(1)}, u32[]{:S(2)}, u32[]{:S(2)}) collective-permute-start(bf16[768,512]{1,0:T(8,128)(2,1)S(1)} %convolution_convert_fusion.5), channel_id=1, source_target_pairs={{0,96},{16,112},{32,0},{48,16},{64,32},{80,48},{96,64},{112,80},{1... | collective-permute-start | bytes 2359304 | tf_op jit(solution)/shard_map/ppermute | solution.py:22
  155.5 10.8 %collective-permute-done.36 = bf16[768,512]{1,0:T(8,128)(2,1)S(1)} collective-permute-done((bf16[768,512]{1,0:T(8,128)(2,1)S(1)}, bf16[768,512]{1,0:T(8,128)(2,1)S(1)}, u32[]{:S(2)}, u32[]{:S(2)}) %collective-permute-start.36) | collective-permute-done | bytes 786464 | tf_op jit(solution)/shard_map/ppermute | solution.py:26
  166.3 1.0 add_convert_fusion
  169.5 1.8 collective-permute-start.39
  171.4 1.0 add_convert_fusion.1
  172.4 2.8 %collective-permute-start.35 = (bf16[768,512]{1,0:T(8,128)(2,1)S(1)}, bf16[768,512]{1,0:T(8,128)(2,1)S(1)}, u32[]{:S(2)}, u32[]{:S(2)}) collective-permute-start(bf16[768,512]{1,0:T(8,128)(2,1)S(1)} %add_convert_fusion.1), channel_id=1, source_target_pairs={{0,16},{16,0},{32,48},{48,32},{64,80},{80,64},{96,112},{112,96},{1... | collective-permute-start | bytes 2359304 | tf_op jit(solution)/shard_map/ppermute | solution.py:26
  175.2 2.3 collective-permute-done.37
  178.6 2.9 %collective-permute-start.40 = (bf16[768,512]{1,0:T(8,128)(2,1)S(1)}, bf16[768,512]{1,0:T(8,128)(2,1)S(1)}, u32[]{:S(2)}, u32[]{:S(2)}) collective-permute-start(bf16[768,512]{1,0:T(8,128)(2,1)S(1)} %pad_maximum_fusion.1), channel_id=1, source_target_pairs={{0,96},{16,112},{32,0},{48,16},{64,32},{80,48},{96,64},{112,80},{1... | collective-permute-start | bytes 2359304 | tf_op jit(solution)/shard_map/ppermute | solution.py:22
  182.5 8.3 %collective-permute-done.35 = bf16[768,512]{1,0:T(8,128)(2,1)S(1)} collective-permute-done((bf16[768,512]{1,0:T(8,128)(2,1)S(1)}, bf16[768,512]{1,0:T(8,128)(2,1)S(1)}, u32[]{:S(2)}, u32[]{:S(2)}) %collective-permute-start.35) | collective-permute-done | bytes 786464 | tf_op jit(solution)/shard_map/ppermute | solution.py:26
  190.8 4.5 %collective-permute-done.38 = bf16[768,512]{1,0:T(8,128)(2,1)S(1)} collective-permute-done((bf16[768,512]{1,0:T(8,128)(2,1)S(1)}, bf16[768,512]{1,0:T(8,128)(2,1)S(1)}, u32[]{:S(2)}, u32[]{:S(2)}) %collective-permute-start.38) | collective-permute-done | bytes 786464 | tf_op jit(solution)/shard_map/ppermute | solution.py:22
  196.3 3.5 %collective-permute-start.46 = (bf16[768,256]{1,0:T(8,128)(2,1)S(1)}, bf16[768,256]{1,0:T(8,128)(2,1)S(1)}, u32[]{:S(2)}, u32[]{:S(2)}) collective-permute-start(bf16[768,256]{1,0:T(8,128)(2,1)S(1)} %fusion.26.refs_0_), channel_id=1, source_target_pairs={{0,96},{16,112},{32,0},{48,16},{64,32},{80,48},{96,64},{112,80},{1... | collective-permute-start | bytes 1179656 | tf_op jit(solution)/shard_map/ppermute | solution.py:22
  199.8 2.4 collective-permute-start.41
  202.2 3.1 %collective-permute-done.44.refs_1_ = bf16[768,256]{1,0:T(8,128)(2,1)S(1)} collective-permute-done((bf16[768,256]{1,0:T(8,128)(2,1)S(1)}, bf16[768,256]{1,0:T(8,128)(2,1)S(1)}, u32[]{:S(2)}, u32[]{:S(2)}) %collective-permute-start.44) | collective-permute-done | bytes 393248 | tf_op jit(solution)/shard_map/ppermute | solution.py:22
  205.5 2.7 %collective-permute-start.47 = (bf16[384,256]{1,0:T(8,128)(2,1)S(1)}, bf16[384,256]{1,0:T(8,128)(2,1)S(1)}, u32[]{:S(2)}, u32[]{:S(2)}) collective-permute-start(bf16[384,256]{1,0:T(8,128)(2,1)S(1)} %slice.154), channel_id=1, source_target_pairs={{0,96},{16,112},{32,0},{48,16},{64,32},{80,48},{96,64},{112,80},{1... | collective-permute-start | bytes 589832 | tf_op jit(solution)/shard_map/ppermute | solution.py:22
  208.2 2.7 %collective-permute-start.43 = (bf16[768,256]{1,0:T(8,128)(2,1)S(1)}, bf16[768,256]{1,0:T(8,128)(2,1)S(1)}, u32[]{:S(2)}, u32[]{:S(2)}) collective-permute-start(bf16[768,256]{1,0:T(8,128)(2,1)S(1)} %collective-permute-done.41.refs_3_), channel_id=1, source_target_pairs={{0,96},{16,112},{32,0},{48,16},{64,32},{80,48},{96,64},{112,80},{1... | collective-permute-start | bytes 1179656 | tf_op jit(solution)/shard_map/ppermute | solution.py:22
  211.5 2.4 collective-permute-start.48
  214.0 2.0 copy-done
  216.1 4.3 %shard_map.134.refs_3_ = f32[768,896]{1,0:T(8,128)S(1)} custom-call(s32[5]{0:T(128)S(1)} %stack.143.order_ref, bf16[1,2048,896]{2,1,0:T(8,128)(2,1)S(1)} %copy-done, bf16[768,256]{1,0:T(8,128)(2,1)S(1)} %fusion.26.refs_0_, bf16[768,256]{1,0:T(8,128)(2,1)S(1)} %collective-permute-done.44.refs_1_, bf16[768,256]{1,0:T(8,128)(2,1)S(1)} %collective-permute-done.46.refs_2_, ...), custom_call_target="tpu_custom_call" | custom-call | flops 1761607680 | bytes 7012352 | tf_op jit(solution)/shard_map/pallas_call | solution.py:248
  220.5 4.0 %shard_map.135 = bf16[768,896]{1,0:T(8,128)(2,1)} custom-call(s32[3]{0:T(128)S(1)} %pad_add_fusion.1.order_ref, bf16[1,2048,896]{2,1,0:T(8,128)(2,1)S(1)} %copy-done.1, bf16[768,256]{1,0:T(8,128)(2,1)S(1)} %collective-permute-done.42.refs_0_, bf16[768,256]{1,0:T(8,128)(2,1)S(1)} %collective-permute-done.43.refs_1_, ...), custom_call_target="tpu_custom_call" | custom-call | flops 1056964608 | bytes 5308416 | tf_op jit(solution)/shard_map/pallas_call | solution.py:248
  224.5 14.3 %all-to-all-start.1 = ((bf16[16,48,896]{2,1,0:T(8,128)(2,1)}), bf16[16,48,896]{2,1,0:T(8,128)(2,1)S(1)}, u32[]{:S(2)}, u32[]{:S(2)}) async-start(bf16[16,48,896]{2,1,0:T(8,128)(2,1)} %bitcast.62), calls=%async_computation.1 | async-start | bytes 2752512 | tf_op jit(solution)/shard_map/all_to_all | solution.py:353
  239.0 19.0 %all-to-all-done.1 = bf16[16,48,896]{2,1,0:T(8,128)(2,1)S(1)} async-done(((bf16[16,48,896]{2,1,0:T(8,128)(2,1)}), bf16[16,48,896]{2,1,0:T(8,128)(2,1)S(1)}, u32[]{:S(2)}, u32[]{:S(2)}) %all-to-all-start.1) | async-done | bytes 1376288 | tf_op jit(solution)/shard_map/all_to_all | solution.py:353
  257.9 1.1 convolution_convert_fusion.9
  (180 shorter events, 19.2 us)
Async XLA Ops:
  2.6 25.5 %copy-start.11 = (bf16[256,640]{1,0:T(8,128)(2,1)}, bf16[256,640]{1,0:T(8,128)(2,1)S(1)}, u32[]{:S(2)}) copy-start(bf16[256,640]{1,0:T(8,128)(2,1)S(1)} %pad_maximum_fusion.2.refs_0_) | copy-start | bytes 983044
  2.6 8.6 %collective-permute-start.1 = (bf16[128,640]{1,0:T(8,128)(2,1)S(1)}, bf16[128,640]{1,0:T(8,128)(2,1)S(1)}, u32[]{:S(2)}, u32[]{:S(2)}) collective-permute-start(bf16[128,640]{1,0:T(8,128)(2,1)S(1)} %constant_dynamic-slice_fusion), channel_id=1, source_target_pairs={{0,32},{16,48},{32,64},{48,80},{64,96},{80,112},{96,0},{112,16},{1... | collective-permute-start | bytes 491528 | tf_op jit(solution)/shard_map/ppermute | solution.py:22
  5.2 6.1 %collective-permute-start.3 = (bf16[128,640]{1,0:T(8,128)(2,1)S(1)}, bf16[128,640]{1,0:T(8,128)(2,1)S(1)}, u32[]{:S(2)}, u32[]{:S(2)}) collective-permute-start(bf16[128,640]{1,0:T(8,128)(2,1)S(1)} %constant_dynamic-slice_fusion), channel_id=1, source_target_pairs={{0,96},{16,112},{32,0},{48,16},{64,32},{80,48},{96,64},{112,80},{1... | collective-permute-start | bytes 491528 | tf_op jit(solution)/shard_map/ppermute | solution.py:22
  7.4 6.7 %collective-permute-start.5 = (bf16[128,640]{1,0:T(8,128)(2,1)S(1)}, bf16[128,640]{1,0:T(8,128)(2,1)S(1)}, u32[]{:S(2)}, u32[]{:S(2)}) collective-permute-start(bf16[128,640]{1,0:T(8,128)(2,1)S(1)} %constant_dynamic-slice_fusion), channel_id=1, source_target_pairs={{0,16},{16,0},{32,48},{48,32},{64,80},{80,64},{96,112},{112,96},{1... | collective-permute-start | bytes 491528 | tf_op jit(solution)/shard_map/ppermute | solution.py:26
  11.2 16.9 %copy-start.22 = (bf16[128,640]{1,0:T(8,128)(2,1)}, bf16[128,640]{1,0:T(8,128)(2,1)S(1)}, u32[]{:S(2)}) copy-start(bf16[128,640]{1,0:T(8,128)(2,1)S(1)} %collective-permute-done.1.refs_1_) | copy-start | bytes 491524
  11.2 6.7 %collective-permute-start.11 = (bf16[64,640]{1,0:T(8,128)(2,1)S(1)}, bf16[64,640]{1,0:T(8,128)(2,1)S(1)}, u32[]{:S(2)}, u32[]{:S(2)}) collective-permute-start(bf16[64,640]{1,0:T(8,128)(2,1)S(1)} %slice.128), channel_id=1, source_target_pairs={{0,32},{16,48},{32,64},{48,80},{64,96},{80,112},{96,0},{112,16},{1... | collective-permute-start | bytes 245768 | tf_op jit(solution)/shard_map/ppermute | solution.py:22
  11.3 16.8 %copy-start.23 = (bf16[128,640]{1,0:T(8,128)(2,1)}, bf16[128,640]{1,0:T(8,128)(2,1)S(1)}, u32[]{:S(2)}) copy-start(bf16[128,640]{1,0:T(8,128)(2,1)S(1)} %collective-permute-done.3.refs_3_) | copy-start | bytes 491524
  11.3 6.8 %collective-permute-start.12 = (bf16[64,640]{1,0:T(8,128)(2,1)S(1)}, bf16[64,640]{1,0:T(8,128)(2,1)S(1)}, u32[]{:S(2)}, u32[]{:S(2)}) collective-permute-start(bf16[64,640]{1,0:T(8,128)(2,1)S(1)} %slice.129), channel_id=1, source_target_pairs={{0,96},{16,112},{32,0},{48,16},{64,32},{80,48},{96,64},{112,80},{1... | collective-permute-start | bytes 245768 | tf_op jit(solution)/shard_map/ppermute | solution.py:22
  14.0 14.0 %copy-start.27 = (bf16[128,640]{1,0:T(8,128)(2,1)}, bf16[128,640]{1,0:T(8,128)(2,1)S(1)}, u32[]{:S(2)}) copy-start(bf16[128,640]{1,0:T(8,128)(2,1)S(1)} %collective-permute-done.5.refs_5_) | copy-start | bytes 491524
  14.1 7.3 %collective-permute-start.9 = (bf16[128,640]{1,0:T(8,128)(2,1)S(1)}, bf16[128,640]{1,0:T(8,128)(2,1)S(1)}, u32[]{:S(2)}, u32[]{:S(2)}) collective-permute-start(bf16[128,640]{1,0:T(8,128)(2,1)S(1)} %collective-permute-done.5.refs_5_), channel_id=1, source_target_pairs={{0,96},{16,112},{32,0},{48,16},{64,32},{80,48},{96,64},{112,80},{1... | collective-permute-start | bytes 491528 | tf_op jit(solution)/shard_map/ppermute | solution.py:22
  14.4 7.5 %collective-permute-start.7 = (bf16[128,640]{1,0:T(8,128)(2,1)S(1)}, bf16[128,640]{1,0:T(8,128)(2,1)S(1)}, u32[]{:S(2)}, u32[]{:S(2)}) collective-permute-start(bf16[128,640]{1,0:T(8,128)(2,1)S(1)} %collective-permute-done.5.refs_5_), channel_id=1, source_target_pairs={{0,32},{16,48},{32,64},{48,80},{64,96},{80,112},{96,0},{112,16},{1... | collective-permute-start | bytes 491528 | tf_op jit(solution)/shard_map/ppermute | solution.py:22
  15.5 8.2 %collective-permute-start.6 = (bf16[128,640]{1,0:T(8,128)(2,1)S(1)}, bf16[128,640]{1,0:T(8,128)(2,1)S(1)}, u32[]{:S(2)}, u32[]{:S(2)}) collective-permute-start(bf16[128,640]{1,0:T(8,128)(2,1)S(1)} %collective-permute-done.5.refs_5_), channel_id=1, source_target_pairs={{0,1},{1,0},{2,3},{3,2},{4,5},{5,4},{6,7},{7,6},{8,9},{9,8},{10,11... | collective-permute-start | bytes 491528 | tf_op jit(solution)/shard_map/ppermute | solution.py:39
  17.9 5.9 %collective-permute-start.2 = (bf16[128,640]{1,0:T(8,128)(2,1)S(1)}, bf16[128,640]{1,0:T(8,128)(2,1)S(1)}, u32[]{:S(2)}, u32[]{:S(2)}) collective-permute-start(bf16[128,640]{1,0:T(8,128)(2,1)S(1)} %collective-permute-done.1.refs_1_), channel_id=1, source_target_pairs={{0,1},{1,0},{2,3},{3,2},{4,5},{5,4},{6,7},{7,6},{8,9},{9,8},{10,11... | collective-permute-start | bytes 491528 | tf_op jit(solution)/shard_map/ppermute | solution.py:39
  18.2 9.9 %copy-start.24 = (bf16[128,640]{1,0:T(8,128)(2,1)}, bf16[128,640]{1,0:T(8,128)(2,1)S(1)}, u32[]{:S(2)}) copy-start(bf16[128,640]{1,0:T(8,128)(2,1)S(1)} %constant_dynamic-update-slice_fusion.refs_11_) | copy-start | bytes 491524
  18.2 7.2 %collective-permute-start.14 = (bf16[128,640]{1,0:T(8,128)(2,1)S(1)}, bf16[128,640]{1,0:T(8,128)(2,1)}, u32[]{:S(2)}, u32[]{:S(2)}) collective-permute-start(bf16[128,640]{1,0:T(8,128)(2,1)S(1)} %constant_dynamic-update-slice_fusion.refs_11_), channel_id=1, source_target_pairs={{0,16},{16,0},{32,48},{48,32},{64,80},{80,64},{96,112},{112,96},{1... | collective-permute-start | bytes 491528 | tf_op jit(solution)/shard_map/ppermute | solution.py:26
  21.3 6.0 %collective-permute-start.4 = (bf16[128,640]{1,0:T(8,128)(2,1)S(1)}, bf16[128,640]{1,0:T(8,128)(2,1)S(1)}, u32[]{:S(2)}, u32[]{:S(2)}) collective-permute-start(bf16[128,640]{1,0:T(8,128)(2,1)S(1)} %collective-permute-done.3.refs_3_), channel_id=1, source_target_pairs={{0,1},{1,0},{2,3},{3,2},{4,5},{5,4},{6,7},{7,6},{8,9},{9,8},{10,11... | collective-permute-start | bytes 491528 | tf_op jit(solution)/shard_map/ppermute | solution.py:39
  22.0 5.4 %collective-permute-start.13 = (bf16[128,640]{1,0:T(8,128)(2,1)S(1)}, bf16[128,640]{1,0:T(8,128)(2,1)S(1)}, u32[]{:S(2)}, u32[]{:S(2)}) collective-permute-start(bf16[128,640]{1,0:T(8,128)(2,1)S(1)} %constant_dynamic-update-slice_fusion.refs_11_), channel_id=1, source_target_pairs={{0,1},{1,0},{2,3},{3,2},{4,5},{5,4},{6,7},{7,6},{8,9},{9,8},{10,11... | collective-permute-start | bytes 491528 | tf_op jit(solution)/shard_map/ppermute | solution.py:39
  23.7 3.7 %collective-permute-start.10 = (bf16[128,640]{1,0:T(8,128)(2,1)S(1)}, bf16[128,640]{1,0:T(8,128)(2,1)S(1)}, u32[]{:S(2)}, u32[]{:S(2)}) collective-permute-start(bf16[128,640]{1,0:T(8,128)(2,1)S(1)} %collective-permute-done.9.refs_9_), channel_id=1, source_target_pairs={{0,1},{1,0},{2,3},{3,2},{4,5},{5,4},{6,7},{7,6},{8,9},{9,8},{10,11... | collective-permute-start | bytes 491528 | tf_op jit(solution)/shard_map/ppermute | solution.py:39
  23.8 3.6 %collective-permute-start.8 = (bf16[128,640]{1,0:T(8,128)(2,1)S(1)}, bf16[128,640]{1,0:T(8,128)(2,1)S(1)}, u32[]{:S(2)}, u32[]{:S(2)}) collective-permute-start(bf16[128,640]{1,0:T(8,128)(2,1)S(1)} %collective-permute-done.7.refs_7_), channel_id=1, source_target_pairs={{0,1},{1,0},{2,3},{3,2},{4,5},{5,4},{6,7},{7,6},{8,9},{9,8},{10,11... | collective-permute-start | bytes 491528 | tf_op jit(solution)/shard_map/ppermute | solution.py:39
  25.4 2.6 %collective-permute-start.15 = (bf16[128,640]{1,0:T(8,128)(2,1)}, bf16[128,640]{1,0:T(8,128)(2,1)}, u32[]{:S(2)}, u32[]{:S(2)}) collective-permute-start(bf16[128,640]{1,0:T(8,128)(2,1)} %collective-permute-done.14.refs_13_), channel_id=1, source_target_pairs={{0,1},{1,0},{2,3},{3,2},{4,5},{5,4},{6,7},{7,6},{8,9},{9,8},{10,11... | collective-permute-start | bytes 491528 | tf_op jit(solution)/shard_map/ppermute | solution.py:39
  27.3 20.8 %copy-start.2 = (bf16[1024,896]{1,0:T(8,128)(2,1)S(1)}, bf16[1024,896]{1,0:T(8,128)(2,1)}, u32[]{:S(2)}) copy-start(bf16[1024,896]{1,0:T(8,128)(2,1)} %refs_0_.3) | copy-start | bytes 5505028
  47.7 1.8 collective-permute-start.16
  48.1 28.8 %collective-permute-start = (bf16[1024,896]{1,0:T(8,128)(2,1)S(1)}, bf16[1024,896]{1,0:T(8,128)(2,1)}, u32[]{:S(2)}, u32[]{:S(2)}) collective-permute-start(bf16[1024,896]{1,0:T(8,128)(2,1)S(1)} %copy-done.2), channel_id=1, source_target_pairs={{0,1},{1,0},{2,3},{3,2},{4,5},{5,4},{6,7},{7,6},{8,9},{9,8},{10,11... | collective-permute-start | bytes 5505032 | tf_op jit(solution)/shard_map/ppermute | solution.py:39
  49.2 27.3 %copy-start.25 = (s32[128,4]{0,1:T(4,128)S(1)}, s32[128,4]{0,1:T(4,128)}, u32[]{:S(2)}) copy-start(s32[128,4]{0,1:T(4,128)} %param.22) | copy-start | bytes 6148
  49.5 24.0 %copy-start.8 = (bf16[128,2048]{1,0:T(8,128)(2,1)}, bf16[128,2048]{1,0:T(8,128)(2,1)S(1)}, u32[]{:S(2)}) copy-start(bf16[128,2048]{1,0:T(8,128)(2,1)S(1)} %constant_dynamic-update-slice_fusion.2.refs_2_) | copy-start | bytes 1572868
  49.5 14.5 %collective-permute-start.20 = (bf16[128,2048]{1,0:T(8,128)(2,1)S(1)}, bf16[128,2048]{1,0:T(8,128)(2,1)S(1)}, u32[]{:S(2)}, u32[]{:S(2)}) collective-permute-start(bf16[128,2048]{1,0:T(8,128)(2,1)S(1)} %constant_dynamic-update-slice_fusion.2.refs_2_), channel_id=1, source_target_pairs={{0,32},{16,48},{32,64},{48,80},{64,96},{80,112},{96,0},{112,16},{1... | collective-permute-start | bytes 1572872 | tf_op jit(solution)/shard_map/ppermute | solution.py:22
  49.6 14.6 %collective-permute-start.22 = (bf16[128,2048]{1,0:T(8,128)(2,1)S(1)}, bf16[128,2048]{1,0:T(8,128)(2,1)S(1)}, u32[]{:S(2)}, u32[]{:S(2)}) collective-permute-start(bf16[128,2048]{1,0:T(8,128)(2,1)S(1)} %constant_dynamic-update-slice_fusion.2.refs_2_), channel_id=1, source_target_pairs={{0,96},{16,112},{32,0},{48,16},{64,32},{80,48},{96,64},{112,80},{1... | collective-permute-start | bytes 1572872 | tf_op jit(solution)/shard_map/ppermute | solution.py:22
  52.3 14.7 %collective-permute-start.17 = (bf16[128,2048]{1,0:T(8,128)(2,1)S(1)}, bf16[128,2048]{1,0:T(8,128)(2,1)}, u32[]{:S(2)}, u32[]{:S(2)}) collective-permute-start(bf16[128,2048]{1,0:T(8,128)(2,1)S(1)} %constant_dynamic-update-slice_fusion.2.refs_2_), channel_id=1, source_target_pairs={{0,16},{16,0},{32,48},{48,32},{64,80},{80,64},{96,112},{112,96},{1... | collective-permute-start | bytes 1572872 | tf_op jit(solution)/shard_map/ppermute | solution.py:26
  64.0 8.7 %copy-start.4 = (bf16[128,2048]{1,0:T(8,128)(2,1)}, bf16[128,2048]{1,0:T(8,128)(2,1)S(1)}, u32[]{:S(2)}) copy-start(bf16[128,2048]{1,0:T(8,128)(2,1)S(1)} %collective-permute-done.20.refs_3_) | copy-start | bytes 1572868
  64.1 8.0 %collective-permute-start.21 = (bf16[64,2048]{1,0:T(8,128)(2,1)S(1)}, bf16[64,2048]{1,0:T(8,128)(2,1)S(1)}, u32[]{:S(2)}, u32[]{:S(2)}) collective-permute-start(bf16[64,2048]{1,0:T(8,128)(2,1)S(1)} %slice.130), channel_id=1, source_target_pairs={{0,32},{16,48},{32,64},{48,80},{64,96},{80,112},{96,0},{112,16},{1... | collective-permute-start | bytes 786440 | tf_op jit(solution)/shard_map/ppermute | solution.py:22
  64.2 9.4 %copy-start.6 = (bf16[128,2048]{1,0:T(8,128)(2,1)}, bf16[128,2048]{1,0:T(8,128)(2,1)S(1)}, u32[]{:S(2)}) copy-start(bf16[128,2048]{1,0:T(8,128)(2,1)S(1)} %collective-permute-done.22.refs_4_) | copy-start | bytes 1572868
  64.2 8.6 %collective-permute-start.23 = (bf16[64,2048]{1,0:T(8,128)(2,1)S(1)}, bf16[64,2048]{1,0:T(8,128)(2,1)S(1)}, u32[]{:S(2)}, u32[]{:S(2)}) collective-permute-start(bf16[64,2048]{1,0:T(8,128)(2,1)S(1)} %slice.131), channel_id=1, source_target_pairs={{0,96},{16,112},{32,0},{48,16},{64,32},{80,48},{96,64},{112,80},{1... | collective-permute-start | bytes 786440 | tf_op jit(solution)/shard_map/ppermute | solution.py:22
  66.9 18.7 %collective-permute-start.18 = (bf16[128,2048]{1,0:T(8,128)(2,1)}, bf16[128,2048]{1,0:T(8,128)(2,1)S(1)}, u32[]{:S(2)}, u32[]{:S(2)}) collective-permute-start(bf16[128,2048]{1,0:T(8,128)(2,1)} %collective-permute-done.17.refs_5_), channel_id=1, source_target_pairs={{0,32},{16,48},{32,64},{48,80},{64,96},{80,112},{96,0},{112,16},{1... | collective-permute-start | bytes 1572872 | tf_op jit(solution)/shard_map/ppermute | solution.py:22
  66.9 18.7 %collective-permute-start.19 = (bf16[128,2048]{1,0:T(8,128)(2,1)}, bf16[128,2048]{1,0:T(8,128)(2,1)S(1)}, u32[]{:S(2)}, u32[]{:S(2)}) collective-permute-start(bf16[128,2048]{1,0:T(8,128)(2,1)} %collective-permute-done.17.refs_5_), channel_id=1, source_target_pairs={{0,96},{16,112},{32,0},{48,16},{64,32},{80,48},{96,64},{112,80},{1... | collective-permute-start | bytes 1572872 | tf_op jit(solution)/shard_map/ppermute | solution.py:22
  73.5 12.1 %collective-permute-start.24 = (bf16[128,2048]{1,0:T(8,128)(2,1)}, bf16[128,2048]{1,0:T(8,128)(2,1)S(1)}, u32[]{:S(2)}, u32[]{:S(2)}) collective-permute-start(bf16[128,2048]{1,0:T(8,128)(2,1)} %constant_dynamic-update-slice_fusion.4.refs_6_), channel_id=1, source_target_pairs={{0,16},{16,0},{32,48},{48,32},{64,80},{80,64},{96,112},{112,96},{1... | collective-permute-start | bytes 1572872 | tf_op jit(solution)/shard_map/ppermute | solution.py:26
  89.7 6.2 %collective-permute-start.25 = (bf16[128,896]{1,0:T(8,128)(2,1)S(1)}, bf16[128,896]{1,0:T(8,128)(2,1)S(1)}, u32[]{:S(2)}, u32[]{:S(2)}) collective-permute-start(bf16[128,896]{1,0:T(8,128)(2,1)S(1)} %get-tuple-element.24), channel_id=1, source_target_pairs={{0,4},{1,5},{2,6},{3,7},{4,8},{5,9},{6,10},{7,11},{8,12},{9,13},{1... | collective-permute-start | bytes 688136 | tf_op jit(solution)/shard_map/ppermute | solution.py:31
  90.9 5.0 %collective-permute-start.26 = (bf16[128,896]{1,0:T(8,128)(2,1)S(1)}, bf16[128,896]{1,0:T(8,128)(2,1)S(1)}, u32[]{:S(2)}, u32[]{:S(2)}) collective-permute-start(bf16[128,896]{1,0:T(8,128)(2,1)S(1)} %get-tuple-element.26), channel_id=1, source_target_pairs={{0,12},{1,13},{2,14},{3,15},{4,0},{5,1},{6,2},{7,3},{8,4},{9,5},{1... | collective-permute-start | bytes 688136 | tf_op jit(solution)/shard_map/ppermute | solution.py:31
  92.4 4.9 %collective-permute-start.28 = (bf16[128,896]{1,0:T(8,128)(2,1)S(1)}, bf16[128,896]{1,0:T(8,128)(2,1)S(1)}, u32[]{:S(2)}, u32[]{:S(2)}) collective-permute-start(bf16[128,896]{1,0:T(8,128)(2,1)S(1)} %get-tuple-element.25), channel_id=1, source_target_pairs={{0,2},{1,3},{2,0},{3,1},{4,6},{5,7},{6,4},{7,5},{8,10},{9,11},{10,... | collective-permute-start | bytes 688136 | tf_op jit(solution)/shard_map/ppermute | solution.py:35
  97.5 4.9 %collective-permute-start.29 = (bf16[64,896]{1,0:T(8,128)(2,1)S(1)}, bf16[64,896]{1,0:T(8,128)(2,1)S(1)}, u32[]{:S(2)}, u32[]{:S(2)}) collective-permute-start(bf16[64,896]{1,0:T(8,128)(2,1)S(1)} %get-tuple-element.33), channel_id=1, source_target_pairs={{0,4},{1,5},{2,6},{3,7},{4,8},{5,9},{6,10},{7,11},{8,12},{9,13},{1... | collective-permute-start | bytes 344072 | tf_op jit(solution)/shard_map/ppermute | solution.py:31
  97.6 4.8 %collective-permute-start.31 = (bf16[64,896]{1,0:T(8,128)(2,1)S(1)}, bf16[64,896]{1,0:T(8,128)(2,1)S(1)}, u32[]{:S(2)}, u32[]{:S(2)}) collective-permute-start(bf16[64,896]{1,0:T(8,128)(2,1)S(1)} %get-tuple-element.34), channel_id=1, source_target_pairs={{0,12},{1,13},{2,14},{3,15},{4,0},{5,1},{6,2},{7,3},{8,4},{9,5},{1... | collective-permute-start | bytes 344072 | tf_op jit(solution)/shard_map/ppermute | solution.py:31
  100.3 5.4 %collective-permute-start.27 = (bf16[128,896]{1,0:T(8,128)(2,1)S(1)}, bf16[128,896]{1,0:T(8,128)(2,1)S(1)}, u32[]{:S(2)}, u32[]{:S(2)}) collective-permute-start(bf16[128,896]{1,0:T(8,128)(2,1)S(1)} %get-tuple-element.22), channel_id=1, source_target_pairs={{0,2},{1,3},{2,0},{3,1},{4,6},{5,7},{6,4},{7,5},{8,10},{9,11},{10,... | collective-permute-start | bytes 688136 | tf_op jit(solution)/shard_map/ppermute | solution.py:35
  102.5 7.5 %collective-permute-start.30 = (bf16[128,896]{1,0:T(8,128)(2,1)S(1)}, bf16[128,896]{1,0:T(8,128)(2,1)S(1)}, u32[]{:S(2)}, u32[]{:S(2)}) collective-permute-start(bf16[128,896]{1,0:T(8,128)(2,1)S(1)} %pad_maximum_fusion.3), channel_id=1, source_target_pairs={{0,4},{1,5},{2,6},{3,7},{4,8},{5,9},{6,10},{7,11},{8,12},{9,13},{1... | collective-permute-start | bytes 688136 | tf_op jit(solution)/shard_map/ppermute | solution.py:31
  103.7 6.4 %collective-permute-start.32 = (bf16[128,896]{1,0:T(8,128)(2,1)S(1)}, bf16[128,896]{1,0:T(8,128)(2,1)S(1)}, u32[]{:S(2)}, u32[]{:S(2)}) collective-permute-start(bf16[128,896]{1,0:T(8,128)(2,1)S(1)} %pad_maximum_fusion.4), channel_id=1, source_target_pairs={{0,12},{1,13},{2,14},{3,15},{4,0},{5,1},{6,2},{7,3},{8,4},{9,5},{1... | collective-permute-start | bytes 688136 | tf_op jit(solution)/shard_map/ppermute | solution.py:31
  111.8 32.5 %all-to-all-start = ((bf16[16,48,896]{2,1,0:T(8,128)(2,1)}), bf16[16,48,896]{2,1,0:T(8,128)(2,1)S(1)}, u32[]{:S(2)}, u32[]{:S(2)}) async-start(bf16[16,48,896]{2,1,0:T(8,128)(2,1)} %bitcast.39), calls=%async_computation | async-start | bytes 2752512 | tf_op jit(solution)/shard_map/all_to_all | solution.py:335
  146.5 19.8 %collective-permute-start.36 = (bf16[768,512]{1,0:T(8,128)(2,1)S(1)}, bf16[768,512]{1,0:T(8,128)(2,1)S(1)}, u32[]{:S(2)}, u32[]{:S(2)}) collective-permute-start(bf16[768,512]{1,0:T(8,128)(2,1)S(1)} %convolution_convert_fusion.2), channel_id=1, source_target_pairs={{0,16},{16,0},{32,48},{48,32},{64,80},{80,64},{96,112},{112,96},{1... | collective-permute-start | bytes 2359304 | tf_op jit(solution)/shard_map/ppermute | solution.py:26
  150.5 20.9 %collective-permute-start.33 = (bf16[768,512]{1,0:T(8,128)(2,1)S(1)}, bf16[768,512]{1,0:T(8,128)(2,1)S(1)}, u32[]{:S(2)}, u32[]{:S(2)}) collective-permute-start(bf16[768,512]{1,0:T(8,128)(2,1)S(1)} %convolution_convert_fusion.6), channel_id=1, source_target_pairs={{0,32},{16,48},{32,64},{48,80},{64,96},{80,112},{96,0},{112,16},{1... | collective-permute-start | bytes 2359304 | tf_op jit(solution)/shard_map/ppermute | solution.py:22
  151.6 19.7 %collective-permute-start.34 = (bf16[768,512]{1,0:T(8,128)(2,1)S(1)}, bf16[768,512]{1,0:T(8,128)(2,1)S(1)}, u32[]{:S(2)}, u32[]{:S(2)}) collective-permute-start(bf16[768,512]{1,0:T(8,128)(2,1)S(1)} %convolution_convert_fusion.5), channel_id=1, source_target_pairs={{0,96},{16,112},{32,0},{48,16},{64,32},{80,48},{96,64},{112,80},{1... | collective-permute-start | bytes 2359304 | tf_op jit(solution)/shard_map/ppermute | solution.py:22
  154.6 11.8 %copy-start.14 = (bf16[896,256]{1,0:T(8,128)(2,1)S(1)}, bf16[896,256]{1,0:T(8,128)(2,1)}, u32[]{:S(2)}) copy-start(bf16[896,256]{1,0:T(8,128)(2,1)} %get-tuple-element.15) | copy-start | bytes 1376260
  154.6 11.8 %copy-start.15 = (bf16[896,256]{1,0:T(8,128)(2,1)S(1)}, bf16[896,256]{1,0:T(8,128)(2,1)}, u32[]{:S(2)}) copy-start(bf16[896,256]{1,0:T(8,128)(2,1)} %get-tuple-element.41) | copy-start | bytes 1376260
  167.4 10.1 %collective-permute-start.37 = (bf16[384,512]{1,0:T(8,128)(2,1)S(1)}, bf16[384,512]{1,0:T(8,128)(2,1)S(1)}, u32[]{:S(2)}, u32[]{:S(2)}) collective-permute-start(bf16[384,512]{1,0:T(8,128)(2,1)S(1)} %get-tuple-element.31), channel_id=1, source_target_pairs={{0,32},{16,48},{32,64},{48,80},{64,96},{80,112},{96,0},{112,16},{1... | collective-permute-start | bytes 1179656 | tf_op jit(solution)/shard_map/ppermute | solution.py:22
  169.5 8.9 %collective-permute-start.39 = (bf16[384,512]{1,0:T(8,128)(2,1)S(1)}, bf16[384,512]{1,0:T(8,128)(2,1)S(1)}, u32[]{:S(2)}, u32[]{:S(2)}) collective-permute-start(bf16[384,512]{1,0:T(8,128)(2,1)S(1)} %get-tuple-element.32), channel_id=1, source_target_pairs={{0,96},{16,112},{32,0},{48,16},{64,32},{80,48},{96,64},{112,80},{1... | collective-permute-start | bytes 1179656 | tf_op jit(solution)/shard_map/ppermute | solution.py:22
  172.4 18.4 %collective-permute-start.35 = (bf16[768,512]{1,0:T(8,128)(2,1)S(1)}, bf16[768,512]{1,0:T(8,128)(2,1)S(1)}, u32[]{:S(2)}, u32[]{:S(2)}) collective-permute-start(bf16[768,512]{1,0:T(8,128)(2,1)S(1)} %add_convert_fusion.1), channel_id=1, source_target_pairs={{0,16},{16,0},{32,48},{48,32},{64,80},{80,64},{96,112},{112,96},{1... | collective-permute-start | bytes 2359304 | tf_op jit(solution)/shard_map/ppermute | solution.py:26
  177.7 17.6 %collective-permute-start.38 = (bf16[768,512]{1,0:T(8,128)(2,1)S(1)}, bf16[768,512]{1,0:T(8,128)(2,1)S(1)}, u32[]{:S(2)}, u32[]{:S(2)}) collective-permute-start(bf16[768,512]{1,0:T(8,128)(2,1)S(1)} %pad_maximum_fusion), channel_id=1, source_target_pairs={{0,32},{16,48},{32,64},{48,80},{64,96},{80,112},{96,0},{112,16},{1... | collective-permute-start | bytes 2359304 | tf_op jit(solution)/shard_map/ppermute | solution.py:22
  178.6 16.9 %collective-permute-start.40 = (bf16[768,512]{1,0:T(8,128)(2,1)S(1)}, bf16[768,512]{1,0:T(8,128)(2,1)S(1)}, u32[]{:S(2)}, u32[]{:S(2)}) collective-permute-start(bf16[768,512]{1,0:T(8,128)(2,1)S(1)} %pad_maximum_fusion.1), channel_id=1, source_target_pairs={{0,96},{16,112},{32,0},{48,16},{64,32},{80,48},{96,64},{112,80},{1... | collective-permute-start | bytes 2359304 | tf_op jit(solution)/shard_map/ppermute | solution.py:22
  196.2 9.2 %collective-permute-start.44 = (bf16[768,256]{1,0:T(8,128)(2,1)S(1)}, bf16[768,256]{1,0:T(8,128)(2,1)S(1)}, u32[]{:S(2)}, u32[]{:S(2)}) collective-permute-start(bf16[768,256]{1,0:T(8,128)(2,1)S(1)} %fusion.26.refs_0_), channel_id=1, source_target_pairs={{0,32},{16,48},{32,64},{48,80},{64,96},{80,112},{96,0},{112,16},{1... | collective-permute-start | bytes 1179656 | tf_op jit(solution)/shard_map/ppermute | solution.py:22
  196.3 9.2 %collective-permute-start.46 = (bf16[768,256]{1,0:T(8,128)(2,1)S(1)}, bf16[768,256]{1,0:T(8,128)(2,1)S(1)}, u32[]{:S(2)}, u32[]{:S(2)}) collective-permute-start(bf16[768,256]{1,0:T(8,128)(2,1)S(1)} %fusion.26.refs_0_), channel_id=1, source_target_pairs={{0,96},{16,112},{32,0},{48,16},{64,32},{80,48},{96,64},{112,80},{1... | collective-permute-start | bytes 1179656 | tf_op jit(solution)/shard_map/ppermute | solution.py:22
  199.8 8.4 %collective-permute-start.41 = (bf16[768,256]{1,0:T(8,128)(2,1)S(1)}, bf16[768,256]{1,0:T(8,128)(2,1)S(1)}, u32[]{:S(2)}, u32[]{:S(2)}) collective-permute-start(bf16[768,256]{1,0:T(8,128)(2,1)S(1)} %fusion.26.refs_0_), channel_id=1, source_target_pairs={{0,16},{16,0},{32,48},{48,32},{64,80},{80,64},{96,112},{112,96},{1... | collective-permute-start | bytes 1179656 | tf_op jit(solution)/shard_map/ppermute | solution.py:26
  205.4 6.1 %collective-permute-start.45 = (bf16[384,256]{1,0:T(8,128)(2,1)S(1)}, bf16[384,256]{1,0:T(8,128)(2,1)S(1)}, u32[]{:S(2)}, u32[]{:S(2)}) collective-permute-start(bf16[384,256]{1,0:T(8,128)(2,1)S(1)} %slice.153), channel_id=1, source_target_pairs={{0,32},{16,48},{32,64},{48,80},{64,96},{80,112},{96,0},{112,16},{1... | collective-permute-start | bytes 589832 | tf_op jit(solution)/shard_map/ppermute | solution.py:22
  205.5 6.0 %collective-permute-start.47 = (bf16[384,256]{1,0:T(8,128)(2,1)S(1)}, bf16[384,256]{1,0:T(8,128)(2,1)S(1)}, u32[]{:S(2)}, u32[]{:S(2)}) collective-permute-start(bf16[384,256]{1,0:T(8,128)(2,1)S(1)} %slice.154), channel_id=1, source_target_pairs={{0,96},{16,112},{32,0},{48,16},{64,32},{80,48},{96,64},{112,80},{1... | collective-permute-start | bytes 589832 | tf_op jit(solution)/shard_map/ppermute | solution.py:22
  208.2 12.2 %collective-permute-start.42 = (bf16[768,256]{1,0:T(8,128)(2,1)S(1)}, bf16[768,256]{1,0:T(8,128)(2,1)S(1)}, u32[]{:S(2)}, u32[]{:S(2)}) collective-permute-start(bf16[768,256]{1,0:T(8,128)(2,1)S(1)} %collective-permute-done.41.refs_3_), channel_id=1, source_target_pairs={{0,32},{16,48},{32,64},{48,80},{64,96},{80,112},{96,0},{112,16},{1... | collective-permute-start | bytes 1179656 | tf_op jit(solution)/shard_map/ppermute | solution.py:22
  208.2 12.2 %collective-permute-start.43 = (bf16[768,256]{1,0:T(8,128)(2,1)S(1)}, bf16[768,256]{1,0:T(8,128)(2,1)S(1)}, u32[]{:S(2)}, u32[]{:S(2)}) collective-permute-start(bf16[768,256]{1,0:T(8,128)(2,1)S(1)} %collective-permute-done.41.refs_3_), channel_id=1, source_target_pairs={{0,96},{16,112},{32,0},{48,16},{64,32},{80,48},{96,64},{112,80},{1... | collective-permute-start | bytes 1179656 | tf_op jit(solution)/shard_map/ppermute | solution.py:22
  211.5 8.9 %collective-permute-start.48 = (bf16[768,256]{1,0:T(8,128)(2,1)S(1)}, bf16[768,256]{1,0:T(8,128)(2,1)S(1)}, u32[]{:S(2)}, u32[]{:S(2)}) collective-permute-start(bf16[768,256]{1,0:T(8,128)(2,1)S(1)} %constant_dynamic-update-slice_fusion.6.refs_4_), channel_id=1, source_target_pairs={{0,16},{16,0},{32,48},{48,32},{64,80},{80,64},{96,112},{112,96},{1... | collective-permute-start | bytes 1179656 | tf_op jit(solution)/shard_map/ppermute | solution.py:26
  224.5 14.3 %copy-start.26 = (bf16[128,4]{0,1:T(4,128)(2,1)S(1)}, bf16[128,4]{0,1:T(4,128)(2,1)}, u32[]{:S(2)}) copy-start(bf16[128,4]{0,1:T(4,128)(2,1)} %param.23) | copy-start | bytes 3076
  224.5 33.5 %all-to-all-start.1 = ((bf16[16,48,896]{2,1,0:T(8,128)(2,1)}), bf16[16,48,896]{2,1,0:T(8,128)(2,1)S(1)}, u32[]{:S(2)}, u32[]{:S(2)}) async-start(bf16[16,48,896]{2,1,0:T(8,128)(2,1)} %bitcast.62), calls=%async_computation.1 | async-start | bytes 2752512 | tf_op jit(solution)/shard_map/all_to_all | solution.py:353
  (23 other events, 67.3 us)
where the time goes:
time: 264 us; the launch traced here: 259 us
  starting transfers between devices  101 us (38%)
  waiting for transfers between devices  85.2 us (32%)
  Pallas kernels  37.2 us (14%)
  local copies, waits for them, and re-layouts  17.4 us (7%)
  matrix products  11.8 us (4%)
  other arithmetic  4.86 us (2%)
    ppermute x24, starting transfers between devices, z_shift(): return lax.ppermute(array, 'ctx', perm)  34.1 us
    ppermute x24, waiting for transfers between devices, z_shift(): return lax.ppermute(array, 'ctx', perm)  23.7 us
    ppermute x8, starting transfers between devices, y_swap(): return lax.ppermute(array, 'ctx', [(i, i ^ 1) for i in range(2 * ZS)])  22.4 us
    ppermute x8, waiting for transfers between devices, y_swap(): return lax.ppermute(array, 'ctx', [(i, i ^ 1) for i in range(2 * ZS)])  20.3 us
    pallas_call x1, Pallas kernels, attention(): pl.pallas_call(functools.partial(attention_kernel, scale=1.0 / math.sqrt(...  19.5 us
    all_to_all x1, waiting for transfers between devices, local(): lax.all_to_all(expert_out, 'exp', split_axis=0, concat_axis=0, tiled=True)  19 us
    all_to_all x1, starting transfers between devices, local(): lax.all_to_all(expert_out, 'exp', split_axis=0, concat_axis=0, tiled=True)  14.3 us
    all_to_all x1, waiting for transfers between devices, local(): lax.all_to_all(send_rows, 'exp', split_axis=0, concat_axis=0, tiled=True)  13.6 us
  transfers between devices with their start and end apart: 51, of which 19 were waited for; matrix products, arithmetic and copies ran while one was open for 7% of the time, Pallas kernels for 4%

commit v1 on v0

--- a/solution.py
+++ b/solution.py
@@ -49,15 +49,21 @@
 
 
 def gather_blocks(own):
-    return other_blocks(first_blocks(own))
-
-
-def other_blocks(blocks):
-    own, up, down, side = blocks
+    own, up, down, side, side_up, side_down, far, _ = gather_parts(own)
+    far = jnp.concatenate(far, axis=0)
+    return own, up, down, side, side_up, side_down, far, y_swap(far)
+
+
+def gather_parts(own):
     half = own.shape[0] // 2
-    far = jnp.concatenate([z_shift(up[:half], 1), z_shift(down[half:], -1)], axis=0)
+    up, down, side = z_shift(own, 1), z_shift(own, -1), y_swap(own)
+    far = z_shift(up[:half], 1), z_shift(down[half:], -1)
     side_up, side_down = z_shift(side, 1), z_shift(side, -1)
-    return own, up, down, side, side_up, side_down, far, y_swap(far)
+    return own, up, down, side, side_up, side_down, far, tuple(y_swap(part) for part in far)
+
+
+def flat(blocks):
+    return [part for block in blocks for part in (block if isinstance(block, tuple) else (block,))]
 
 
 def add(*terms):
@@ -166,17 +172,19 @@
     )(jnp.append(where, core), q_nope, q_rope, w_uk, w_uv, *pieces)
 
 
-def project_kernel(places_ref, *refs, depths, count, before):
+def project_kernel(places_ref, *refs, depths, count, parts, before):
     weight_refs, refs = refs[: len(depths)], refs[len(depths) :]
-    block_refs, refs = refs[:count], refs[count:]
-    *before_refs, out_ref, weights, blocks, sem = refs
-    rows = block_refs[0].shape[0]
+    *before_refs, out_ref, weights, blocks, sem = refs[parts:]
+    block_refs = refs[:parts]
+    rows = blocks.shape[0] // count
     copies, at = [], 0
     for ref, depth in zip(weight_refs, depths, strict=True):
         copies.append((ref, weights.at[pl.ds(at, depth)]))
         at += depth
-    for n, ref in enumerate(block_refs):
-        copies.append((ref, blocks.at[pl.ds(n * rows, rows)]))
+    at = 0
+    for ref in block_refs:
+        copies.append((ref, blocks.at[pl.ds(at, ref.shape[0])]))
+        at += ref.shape[0]
     copies = [pltpu.make_async_copy(a, b, sem.at[n]) for n, (a, b) in enumerate(copies)]
     for copy in copies:
         copy.start()
@@ -192,43 +200,49 @@
 
 
 def project(weights, blocks, places, earlier=None):
-    rows = blocks[0].shape[0]
+    count, blocks = len(blocks), flat(blocks)
+    rows = sum(b.shape[0] for b in blocks) // count
     columns = weights[0].shape[1]
     depths = [w.shape[0] for w in weights]
     before = 0 if earlier is None else earlier.shape[0]
     vmem = pl.BlockSpec(memory_space=pltpu.VMEM)
-    kernel = functools.partial(project_kernel, depths=depths, count=len(blocks), before=before)
+    kernel = functools.partial(
+        project_kernel, depths=depths, count=count, parts=len(blocks), before=before
+    )
     return pl.pallas_call(
         kernel,
         in_specs=[pl.BlockSpec(memory_space=pltpu.SMEM)]
         + [pl.BlockSpec(memory_space=pl.ANY)] * (len(weights) + len(blocks))
         + [vmem] * (before > 0),
         out_specs=vmem,
-        out_shape=jax.ShapeDtypeStruct((before + len(blocks), rows, columns), BF),
+        out_shape=jax.ShapeDtypeStruct((before + count, rows, columns), BF),
         scratch_shapes=[
             pltpu.VMEM((sum(depths), columns), BF),
-            pltpu.VMEM((len(blocks) * rows, sum(depths)), BF),
+            pltpu.VMEM((count * rows, sum(depths)), BF),
             pltpu.SemaphoreType.DMA((len(weights) + len(blocks),)),
         ],
         compiler_params=pltpu.CompilerParams(vmem_limit_bytes=40 * 2**20),
         cost_estimate=pl.CostEstimate(
-            flops=2 * len(blocks) * rows * sum(depths) * columns,
-            bytes_accessed=2 * (sum(depths) * columns + len(blocks) * rows * (sum(depths) + columns)),
+            flops=2 * count * rows * sum(depths) * columns,
+            bytes_accessed=2 * (sum(depths) * columns + count * rows * (sum(depths) + columns)),
             transcendentals=0,
         ),
     )(places, *weights, *blocks, *([] if earlier is None else [earlier]))
 
 
-def combine_kernel(order_ref, w_ref, *refs, count):
-    block_refs, refs = refs[:count], refs[count:]
-    *before_refs, out_ref, weights, blocks, sem = refs
-    step = block_refs[0].shape[1]
+def combine_kernel(order_ref, w_ref, *refs, count, parts):
+    *before_refs, out_ref, weights, blocks, sem = refs[parts:]
+    step = refs[0].shape[1]
     copies = []
-    for n, ref in enumerate(block_refs):
+    for n in range(count):
         start = pl.multiple_of(order_ref[n] * step, step)
         source = w_ref.at[0, pl.ds(start, step)]
         copies.append((source, weights.at[pl.ds(n * step, step)]))
-        copies.append((ref, blocks.at[:, pl.ds(n * step, step)]))
+    at = 0
+    for ref in refs[:parts]:
+        n, row = at // blocks.shape[0], at % blocks.shape[0]
+        copies.append((ref, blocks.at[pl.ds(row, ref.shape[0]), pl.ds(n * step, step)]))
+        at += ref.shape[0]
     copies = [pltpu.make_async_copy(a, b, sem.at[n]) for n, (a, b) in enumerate(copies)]
     for copy in copies:
         copy.start()
@@ -241,12 +255,13 @@
 
 
 def combine(order, w_down, blocks, dtype, earlier=()):
-    rows, step = blocks[0].shape
+    count, blocks = len(blocks), flat(blocks)
+    rows, step = sum(b.shape[0] for b in blocks) // count, blocks[0].shape[1]
     columns = w_down.shape[2]
-    depth = len(blocks) * step
+    depth = count * step
     vmem = pl.BlockSpec(memory_space=pltpu.VMEM)
     return pl.pallas_call(
-        functools.partial(combine_kernel, count=len(blocks)),
+        functools.partial(combine_kernel, count=count, parts=len(blocks)),
         in_specs=[pl.BlockSpec(memory_space=pltpu.SMEM)]
         + [pl.BlockSpec(memory_space=pl.ANY)] * (1 + len(blocks))
         + [vmem] * len(earlier),
@@ -255,7 +270,7 @@
         scratch_shapes=[
             pltpu.VMEM((depth, columns), BF),
             pltpu.VMEM((rows, depth), BF),
-            pltpu.SemaphoreType.DMA((2 * len(blocks),)),
+            pltpu.SemaphoreType.DMA((count + len(blocks),)),
         ],
         compiler_params=pltpu.CompilerParams(vmem_limit_bytes=40 * 2**20),
         cost_estimate=pl.CostEstimate(
@@ -300,7 +315,7 @@
 
     mine, other = attention(where, core, q_nope, q_rope, pieces, w_uk, w_uv)
 
-    blocks = gather_blocks(jnp.concatenate([mine, core_swap(other)], axis=1))
+    blocks = gather_parts(jnp.concatenate([mine, core_swap(other)], axis=1))
     weights = [w_out, core_swap(w_out)]
     first, last = [0, 1, 2, 3, 6], [4, 5, 7]
     chip = lax.axis_index("exp") // 2
@@ -346,7 +361,7 @@
 
     pre = scatter_sum(part, z_shift, y_swap)
     hidden = (jax.nn.silu(pre[:, :hidden_cols]) * pre[:, hidden_cols:]).astype(BF)
-    all_hidden = gather_blocks(hidden)
+    all_hidden = gather_parts(hidden)
     early = combine([order[b] for b in first], w_down, [all_hidden[b] for b in first], F32)
     expert_out = combine([order[b] for b in last], w_down, [all_hidden[b] for b in last], BF, [early])
     expert_out = expert_out.reshape(expert_count, capacity, feature_cols)

time: 264 us -> 264 us (level)
    ppermute x8 -> x10, starting transfers between devices: 22.4 us -> 23.2 us  [y_swap(): return lax.ppermute(array, 'ctx', [(i, i ^ 1) for i in range(2 * ZS)])]
    ppermute x8 -> x10, waiting for transfers between devices: 20.3 us -> 20.5 us  [y_swap(): return lax.ppermute(array, 'ctx', [(i, i ^ 1) for i in range(2 * ZS)])]
  transfers between devices with their start and end apart: 51 -> 53, of which waited for: 19 -> 18; matrix products, arithmetic and copies ran while one was open for 7% -> 7% of each run, Pallas kernels for 4% -> 11%
where the time goes in v1:
time: 264 us; the launch traced here: 260 us
  starting transfers between devices  102 us (39%)
  waiting for transfers between devices  84.4 us (32%)
  Pallas kernels  37.2 us (14%)
  local copies, waits for them, and re-layouts  16.9 us (6%)
  matrix products  11.7 us (4%)
  other arithmetic  4.81 us (2%)
    ppermute x24, starting transfers between devices, z_shift(): return lax.ppermute(array, 'ctx', perm)  33.8 us
    ppermute x10, starting transfers between devices, y_swap(): return lax.ppermute(array, 'ctx', [(i, i ^ 1) for i in range(2 * ZS)])  23.2 us
    ppermute x24, waiting for transfers between devices, z_shift(): return lax.ppermute(array, 'ctx', perm)  22.9 us
    ppermute x10, waiting for transfers between devices, y_swap(): return lax.ppermute(array, 'ctx', [(i, i ^ 1) for i in range(2 * ZS)])  20.5 us
    pallas_call x1, Pallas kernels, attention(): pl.pallas_call(functools.partial(attention_kernel, scale=1.0 / math.sqrt(...  19.5 us
    all_to_all x1, waiting for transfers between devices, local(): lax.all_to_all(expert_out, 'exp', split_axis=0, concat_axis=0, tiled=True)  19 us
    all_to_all x1, starting transfers between devices, local(): lax.all_to_all(expert_out, 'exp', split_axis=0, concat_axis=0, tiled=True)  14.6 us
    all_to_all x1, waiting for transfers between devices, local(): lax.all_to_all(send_rows, 'exp', split_axis=0, concat_axis=0, tiled=True)  13.6 us
  transfers between devices with their start and end apart: 53, of which 18 were waited for; matrix products, arithmetic and copies ran while one was open for 7% of the time, Pallas kernels for 11%

profile of v1, /device:TPU:1, one launch (start us, length us, event | category | flops | bytes accessed | tf_op | source)
XLA Modules:
  0.0 259.5 jit_solution(10240022922325441523)
XLA Ops:
  0.7 1.0 copy.34
  1.7 1.0 pad_maximum_fusion.2.refs_0_
  2.8 2.5 collective-permute-start.1
  5.3 2.2 collective-permute-start.3
  7.5 2.9 %collective-permute-start.5 = (bf16[128,640]{1,0:T(8,128)(2,1)S(1)}, bf16[128,640]{1,0:T(8,128)(2,1)S(1)}, u32[]{:S(2)}, u32[]{:S(2)}) collective-permute-start(bf16[128,640]{1,0:T(8,128)(2,1)S(1)} %constant_dynamic-slice_fusion), channel_id=1, source_target_pairs={{0,16},{16,0},{32,48},{48,32},{64,80},{80,64},{96,112},{112,96},{1... | collective-permute-start | bytes 491528 | tf_op jit(solution)/shard_map/ppermute | solution.py:26
  11.5 2.7 %collective-permute-start.12 = (bf16[64,640]{1,0:T(8,128)(2,1)S(1)}, bf16[64,640]{1,0:T(8,128)(2,1)S(1)}, u32[]{:S(2)}, u32[]{:S(2)}) collective-permute-start(bf16[64,640]{1,0:T(8,128)(2,1)S(1)} %slice.129), channel_id=1, source_target_pairs={{0,96},{16,112},{32,0},{48,16},{64,32},{80,48},{96,64},{112,80},{1... | collective-permute-start | bytes 245768 | tf_op jit(solution)/shard_map/ppermute | solution.py:22
  14.6 1.1 collective-permute-start.7
  15.7 2.3 collective-permute-start.6
  18.4 3.0 %collective-permute-start.14 = (bf16[128,640]{1,0:T(8,128)(2,1)S(1)}, bf16[128,640]{1,0:T(8,128)(2,1)}, u32[]{:S(2)}, u32[]{:S(2)}) collective-permute-start(bf16[128,640]{1,0:T(8,128)(2,1)S(1)} %constant_dynamic-update-slice_fusion.refs_11_), channel_id=1, source_target_pairs={{0,16},{16,0},{32,48},{48,32},{64,80},{80,64},{96,112},{112,96},{1... | collective-permute-start | bytes 491528 | tf_op jit(solution)/shard_map/ppermute | solution.py:26
  22.1 1.7 collective-permute-start.13
  24.3 1.2 collective-permute-done.14.refs_13_
  25.6 1.1 collective-permute-start.15
  28.5 19.5 %shard_map.131 = (bf16[128,1024]{1,0:T(8,128)(2,1)}, bf16[128,1024]{1,0:T(8,128)(2,1)}) custom-call(s32[17]{0:T(128)} %pad_add_fusion.where_ref, bf16[256,1024]{1,0:T(8,128)(2,1)} %qn_ref.1, bf16[256,512]{1,0:T(8,128)(2,1)} %qr_ref.1, bf16[8,128,512]{2,1,0:T(8,128)(2,1)} %uk_ref.1, bf16[8,512,128]{2,1,0:T(8,128)(2,1)} %uv_ref.1, ...), custom_call_target="tpu_custom_call" | custom-call | flops 9663676416 | bytes 3670016 | tf_op jit(solution)/shard_map/pallas_call | solution.py:150
  50.0 2.7 %collective-permute-start.23 = (bf16[128,2048]{1,0:T(8,128)(2,1)S(1)}, bf16[128,2048]{1,0:T(8,128)(2,1)S(1)}, u32[]{:S(2)}, u32[]{:S(2)}) collective-permute-start(bf16[128,2048]{1,0:T(8,128)(2,1)S(1)} %constant_dynamic-update-slice_fusion.2.refs_2_), channel_id=1, source_target_pairs={{0,96},{16,112},{32,0},{48,16},{64,32},{80,48},{96,64},{112,80},{1... | collective-permute-start | bytes 1572872 | tf_op jit(solution)/shard_map/ppermute | solution.py:22
  52.7 2.9 %collective-permute-start.17 = (bf16[128,2048]{1,0:T(8,128)(2,1)S(1)}, bf16[128,2048]{1,0:T(8,128)(2,1)}, u32[]{:S(2)}, u32[]{:S(2)}) collective-permute-start(bf16[128,2048]{1,0:T(8,128)(2,1)S(1)} %constant_dynamic-update-slice_fusion.2.refs_2_), channel_id=1, source_target_pairs={{0,16},{16,0},{32,48},{48,32},{64,80},{80,64},{96,112},{112,96},{1... | collective-permute-start | bytes 1572872 | tf_op jit(solution)/shard_map/ppermute | solution.py:26
  56.4 8.1 %collective-permute-done.20.refs_3_ = bf16[128,2048]{1,0:T(8,128)(2,1)S(1)} collective-permute-done((bf16[128,2048]{1,0:T(8,128)(2,1)S(1)}, bf16[128,2048]{1,0:T(8,128)(2,1)S(1)}, u32[]{:S(2)}, u32[]{:S(2)}) %collective-permute-start.20) | collective-permute-done | bytes 524320 | tf_op jit(solution)/shard_map/ppermute | solution.py:22
  64.6 2.7 %collective-permute-start.24 = (bf16[64,2048]{1,0:T(8,128)(2,1)S(1)}, bf16[64,2048]{1,0:T(8,128)(2,1)}, u32[]{:S(2)}, u32[]{:S(2)}) collective-permute-start(bf16[64,2048]{1,0:T(8,128)(2,1)S(1)} %slice.131), channel_id=1, source_target_pairs={{0,96},{16,112},{32,0},{48,16},{64,32},{80,48},{96,64},{112,80},{1... | collective-permute-start | bytes 786440 | tf_op jit(solution)/shard_map/ppermute | solution.py:22
  67.4 2.7 %collective-permute-start.19 = (bf16[128,2048]{1,0:T(8,128)(2,1)}, bf16[128,2048]{1,0:T(8,128)(2,1)S(1)}, u32[]{:S(2)}, u32[]{:S(2)}) collective-permute-start(bf16[128,2048]{1,0:T(8,128)(2,1)} %collective-permute-done.17.refs_5_), channel_id=1, source_target_pairs={{0,96},{16,112},{32,0},{48,16},{64,32},{80,48},{96,64},{112,80},{1... | collective-permute-start | bytes 1572872 | tf_op jit(solution)/shard_map/ppermute | solution.py:22
  70.0 2.6 collective-permute-done.21.refs_6_
  72.6 2.7 %collective-permute-start.22 = (bf16[64,2048]{1,0:T(8,128)(2,1)}, bf16[64,2048]{1,0:T(8,128)(2,1)S(1)}, u32[]{:S(2)}, u32[]{:S(2)}) collective-permute-start(bf16[64,2048]{1,0:T(8,128)(2,1)} %collective-permute-done.21.refs_6_), channel_id=1, source_target_pairs={{0,16},{16,0},{32,48},{48,32},{64,80},{80,64},{96,112},{112,96},{1... | collective-permute-start | bytes 786440 | tf_op jit(solution)/shard_map/ppermute | solution.py:26
  76.5 1.2 copy-done.5
  77.7 1.0 copy-done.7
  78.7 1.0 copy-done.9
  79.8 5.3 %shard_map.132.refs_6_ = bf16[5,128,896]{2,1,0:T(8,128)(2,1)S(1)} custom-call(s32[8]{0:T(128)S(1)} %stack.116.places_ref, bf16[1024,896]{1,0:T(8,128)(2,1)S(1)} %copy-done.2, bf16[1024,896]{1,0:T(8,128)(2,1)} %collective-permute-done.refs_1_, bf16[128,2048]{1,0:T(8,128)(2,1)S(1)} %copy-done.9, bf16[128,2048]{1,0:T(8,128)(2,1)S(1)} %copy-done.5, ...), custom_call_target="tpu_custom_call" | custom-call | flops 2348810240 | bytes 7438336 | tf_op jit(solution)/shard_map/pallas_call | solution.py:212
  85.2 4.0 %shard_map.133 = bf16[8,128,896]{2,1,0:T(8,128)(2,1)S(1)} custom-call(s32[8]{0:T(128)S(1)} %stack.116.places_ref, bf16[1024,896]{1,0:T(8,128)(2,1)S(1)} %copy-done.3, bf16[1024,896]{1,0:T(8,128)(2,1)} %collective-permute-done.refs_1_, bf16[128,2048]{1,0:T(8,128)(2,1)S(1)} %collective-permute-done.18.refs_2_, ...), custom_call_target="tpu_custom_call" | custom-call | flops 1409286144 | bytes 5931008 | tf_op jit(solution)/shard_map/pallas_call | solution.py:212
  89.2 1.3 collective-permute-start.26
  90.5 1.4 collective-permute-start.27
  93.0 1.2 reduce-window.6
  95.4 1.4 collective-permute-done.29
  97.1 2.7 %collective-permute-start.32 = (bf16[64,896]{1,0:T(8,128)(2,1)S(1)}, bf16[64,896]{1,0:T(8,128)(2,1)S(1)}, u32[]{:S(2)}, u32[]{:S(2)}) collective-permute-start(bf16[64,896]{1,0:T(8,128)(2,1)S(1)} %get-tuple-element.34), channel_id=1, source_target_pairs={{0,12},{1,13},{2,14},{3,15},{4,0},{5,1},{6,2},{7,3},{8,4},{9,5},{1... | collective-permute-start | bytes 344072 | tf_op jit(solution)/shard_map/ppermute | solution.py:31
  100.8 1.2 collective-permute-done.30
  102.1 1.1 collective-permute-start.31
  103.2 1.7 collective-permute-start.33
  105.2 4.5 %collective-permute-done.31 = bf16[128,896]{1,0:T(8,128)(2,1)S(1)} collective-permute-done((bf16[128,896]{1,0:T(8,128)(2,1)S(1)}, bf16[128,896]{1,0:T(8,128)(2,1)S(1)}, u32[]{:S(2)}, u32[]{:S(2)}) %collective-permute-start.31) | collective-permute-done | bytes 229408 | tf_op jit(solution)/shard_map/ppermute | solution.py:31
  109.8 1.7 convolution_convert_fusion
  111.5 13.3 %all-to-all-start = ((bf16[16,48,896]{2,1,0:T(8,128)(2,1)}), bf16[16,48,896]{2,1,0:T(8,128)(2,1)S(1)}, u32[]{:S(2)}, u32[]{:S(2)}) async-start(bf16[16,48,896]{2,1,0:T(8,128)(2,1)} %bitcast.39), calls=%async_computation | async-start | bytes 2752512 | tf_op jit(solution)/shard_map/all_to_all | solution.py:350
  124.7 5.6 %dynamic-slice_bitcast_fusion.14 = (bf16[896,256]{1,0:T(8,128)(2,1)}, bf16[896,256]{1,0:T(8,128)(2,1)}, bf16[896,256]{1,0:T(8,128)(2,1)S(1)}, bf16[896,256]{1,0:...) fusion(bf16[1,896,2048]{2,1,0:T(8,128)(2,1)} %param.20, ...), kind=kLoop, calls=%fused_computation.70 | loop fusion | bytes 14680096 | tf_op jit(solution)/shard_map/dynamic_slice | solution.py:358
  130.3 13.6 %all-to-all-done = bf16[16,48,896]{2,1,0:T(8,128)(2,1)S(1)} async-done(((bf16[16,48,896]{2,1,0:T(8,128)(2,1)}), bf16[16,48,896]{2,1,0:T(8,128)(2,1)S(1)}, u32[]{:S(2)}, u32[]{:S(2)}) %all-to-all-start) | async-done | bytes 1376288 | tf_op jit(solution)/shard_map/all_to_all | solution.py:350
  143.9 2.1 convolution_convert_fusion.2
  146.0 2.8 %collective-permute-start.37 = (bf16[768,512]{1,0:T(8,128)(2,1)S(1)}, bf16[768,512]{1,0:T(8,128)(2,1)S(1)}, u32[]{:S(2)}, u32[]{:S(2)}) collective-permute-start(bf16[768,512]{1,0:T(8,128)(2,1)S(1)} %convolution_convert_fusion.2), channel_id=1, source_target_pairs={{0,16},{16,0},{32,48},{48,32},{64,80},{80,64},{96,112},{112,96},{1... | collective-permute-start | bytes 2359304 | tf_op jit(solution)/shard_map/ppermute | solution.py:26
  148.8 1.0 convolution_convert_fusion.6
  151.0 2.9 %collective-permute-start.35 = (bf16[768,512]{1,0:T(8,128)(2,1)S(1)}, bf16[768,512]{1,0:T(8,128)(2,1)S(1)}, u32[]{:S(2)}, u32[]{:S(2)}) collective-permute-start(bf16[768,512]{1,0:T(8,128)(2,1)S(1)} %convolution_convert_fusion.5), channel_id=1, source_target_pairs={{0,96},{16,112},{32,0},{48,16},{64,32},{80,48},{96,64},{112,80},{1... | collective-permute-start | bytes 2359304 | tf_op jit(solution)/shard_map/ppermute | solution.py:22
  154.9 10.9 %collective-permute-done.37 = bf16[768,512]{1,0:T(8,128)(2,1)S(1)} collective-permute-done((bf16[768,512]{1,0:T(8,128)(2,1)S(1)}, bf16[768,512]{1,0:T(8,128)(2,1)S(1)}, u32[]{:S(2)}, u32[]{:S(2)}) %collective-permute-start.37) | collective-permute-done | bytes 786464 | tf_op jit(solution)/shard_map/ppermute | solution.py:26
  165.8 1.0 add_convert_fusion
  167.9 1.0 convolution_convert_fusion.1
  169.0 1.8 collective-permute-start.40
  170.8 1.0 add_convert_fusion.1
  171.8 2.8 %collective-permute-start.36 = (bf16[768,512]{1,0:T(8,128)(2,1)S(1)}, bf16[768,512]{1,0:T(8,128)(2,1)S(1)}, u32[]{:S(2)}, u32[]{:S(2)}) collective-permute-start(bf16[768,512]{1,0:T(8,128)(2,1)S(1)} %add_convert_fusion.1), channel_id=1, source_target_pairs={{0,16},{16,0},{32,48},{48,32},{64,80},{80,64},{96,112},{112,96},{1... | collective-permute-start | bytes 2359304 | tf_op jit(solution)/shard_map/ppermute | solution.py:26
  174.6 2.4 collective-permute-done.38
  178.1 2.7 %collective-permute-start.41 = (bf16[768,512]{1,0:T(8,128)(2,1)S(1)}, bf16[768,512]{1,0:T(8,128)(2,1)S(1)}, u32[]{:S(2)}, u32[]{:S(2)}) collective-permute-start(bf16[768,512]{1,0:T(8,128)(2,1)S(1)} %pad_maximum_fusion.1), channel_id=1, source_target_pairs={{0,96},{16,112},{32,0},{48,16},{64,32},{80,48},{96,64},{112,80},{1... | collective-permute-start | bytes 2359304 | tf_op jit(solution)/shard_map/ppermute | solution.py:22
  181.8 8.3 %collective-permute-done.36 = bf16[768,512]{1,0:T(8,128)(2,1)S(1)} collective-permute-done((bf16[768,512]{1,0:T(8,128)(2,1)S(1)}, bf16[768,512]{1,0:T(8,128)(2,1)S(1)}, u32[]{:S(2)}, u32[]{:S(2)}) %collective-permute-start.36) | collective-permute-done | bytes 786464 | tf_op jit(solution)/shard_map/ppermute | solution.py:26
  190.1 4.6 %collective-permute-done.39 = bf16[768,512]{1,0:T(8,128)(2,1)S(1)} collective-permute-done((bf16[768,512]{1,0:T(8,128)(2,1)S(1)}, bf16[768,512]{1,0:T(8,128)(2,1)S(1)}, u32[]{:S(2)}, u32[]{:S(2)}) %collective-permute-start.39) | collective-permute-done | bytes 786464 | tf_op jit(solution)/shard_map/ppermute | solution.py:22
  195.5 3.4 %collective-permute-start.48 = (bf16[768,256]{1,0:T(8,128)(2,1)S(1)}, bf16[768,256]{1,0:T(8,128)(2,1)S(1)}, u32[]{:S(2)}, u32[]{:S(2)}) collective-permute-start(bf16[768,256]{1,0:T(8,128)(2,1)S(1)} %fusion.26.refs_0_), channel_id=1, source_target_pairs={{0,96},{16,112},{32,0},{48,16},{64,32},{80,48},{96,64},{112,80},{1... | collective-permute-start | bytes 1179656 | tf_op jit(solution)/shard_map/ppermute | solution.py:22
  198.9 2.6 collective-permute-start.42
  201.5 2.9 %collective-permute-done.45.refs_1_ = bf16[768,256]{1,0:T(8,128)(2,1)S(1)} collective-permute-done((bf16[768,256]{1,0:T(8,128)(2,1)S(1)}, bf16[768,256]{1,0:T(8,128)(2,1)S(1)}, u32[]{:S(2)}, u32[]{:S(2)}) %collective-permute-start.45) | collective-permute-done | bytes 393248 | tf_op jit(solution)/shard_map/ppermute | solution.py:22
  204.6 2.7 %collective-permute-start.49 = (bf16[384,256]{1,0:T(8,128)(2,1)S(1)}, bf16[384,256]{1,0:T(8,128)(2,1)S(1)}, u32[]{:S(2)}, u32[]{:S(2)}) collective-permute-start(bf16[384,256]{1,0:T(8,128)(2,1)S(1)} %slice.154), channel_id=1, source_target_pairs={{0,96},{16,112},{32,0},{48,16},{64,32},{80,48},{96,64},{112,80},{1... | collective-permute-start | bytes 589832 | tf_op jit(solution)/shard_map/ppermute | solution.py:22
  207.3 2.7 %collective-permute-start.44 = (bf16[768,256]{1,0:T(8,128)(2,1)S(1)}, bf16[768,256]{1,0:T(8,128)(2,1)S(1)}, u32[]{:S(2)}, u32[]{:S(2)}) collective-permute-start(bf16[768,256]{1,0:T(8,128)(2,1)S(1)} %collective-permute-done.42.refs_3_), channel_id=1, source_target_pairs={{0,96},{16,112},{32,0},{48,16},{64,32},{80,48},{96,64},{112,80},{1... | collective-permute-start | bytes 1179656 | tf_op jit(solution)/shard_map/ppermute | solution.py:22
  210.6 2.4 collective-permute-start.47
  213.8 2.0 copy-done
  215.8 4.3 %shard_map.134.refs_4_ = f32[768,896]{1,0:T(8,128)S(1)} custom-call(s32[5]{0:T(128)S(1)} %stack.143.order_ref, bf16[1,2048,896]{2,1,0:T(8,128)(2,1)S(1)} %copy-done, bf16[768,256]{1,0:T(8,128)(2,1)S(1)} %fusion.26.refs_0_, bf16[768,256]{1,0:T(8,128)(2,1)S(1)} %collective-permute-done.45.refs_1_, bf16[768,256]{1,0:T(8,128)(2,1)S(1)} %collective-permute-done.48.refs_2_, ...), custom_call_target="tpu_custom_call" | custom-call | flops 1761607680 | bytes 7012352 | tf_op jit(solution)/shard_map/pallas_call | solution.py:263
  220.2 4.0 %shard_map.135 = bf16[768,896]{1,0:T(8,128)(2,1)} custom-call(s32[3]{0:T(128)S(1)} %pad_add_fusion.1.order_ref, bf16[1,2048,896]{2,1,0:T(8,128)(2,1)S(1)} %copy-done.1, bf16[768,256]{1,0:T(8,128)(2,1)S(1)} %collective-permute-done.43.refs_0_, bf16[768,256]{1,0:T(8,128)(2,1)S(1)} %collective-permute-done.44.refs_1_, ...), custom_call_target="tpu_custom_call" | custom-call | flops 1056964608 | bytes 5308416 | tf_op jit(solution)/shard_map/pallas_call | solution.py:263
  224.3 14.6 %all-to-all-start.1 = ((bf16[16,48,896]{2,1,0:T(8,128)(2,1)}), bf16[16,48,896]{2,1,0:T(8,128)(2,1)S(1)}, u32[]{:S(2)}, u32[]{:S(2)}) async-start(bf16[16,48,896]{2,1,0:T(8,128)(2,1)} %bitcast.62), calls=%async_computation.1 | async-start | bytes 2752512 | tf_op jit(solution)/shard_map/all_to_all | solution.py:368
  239.0 19.0 %all-to-all-done.1 = bf16[16,48,896]{2,1,0:T(8,128)(2,1)S(1)} async-done(((bf16[16,48,896]{2,1,0:T(8,128)(2,1)}), bf16[16,48,896]{2,1,0:T(8,128)(2,1)S(1)}, u32[]{:S(2)}, u32[]{:S(2)}) %all-to-all-start.1) | async-done | bytes 1376288 | tf_op jit(solution)/shard_map/all_to_all | solution.py:368
  258.0 1.1 convolution_convert_fusion.9
  (182 shorter events, 20.3 us)
Async XLA Ops:
  0.6 26.7 %copy-start.2 = (bf16[1024,896]{1,0:T(8,128)(2,1)S(1)}, bf16[1024,896]{1,0:T(8,128)(2,1)}, u32[]{:S(2)}) copy-start(bf16[1024,896]{1,0:T(8,128)(2,1)} %refs_0_.3) | copy-start | bytes 5505028
  2.7 25.7 %copy-start.11 = (bf16[256,640]{1,0:T(8,128)(2,1)}, bf16[256,640]{1,0:T(8,128)(2,1)S(1)}, u32[]{:S(2)}) copy-start(bf16[256,640]{1,0:T(8,128)(2,1)S(1)} %pad_maximum_fusion.2.refs_0_) | copy-start | bytes 983044
  2.8 8.6 %collective-permute-start.1 = (bf16[128,640]{1,0:T(8,128)(2,1)S(1)}, bf16[128,640]{1,0:T(8,128)(2,1)S(1)}, u32[]{:S(2)}, u32[]{:S(2)}) collective-permute-start(bf16[128,640]{1,0:T(8,128)(2,1)S(1)} %constant_dynamic-slice_fusion), channel_id=1, source_target_pairs={{0,32},{16,48},{32,64},{48,80},{64,96},{80,112},{96,0},{112,16},{1... | collective-permute-start | bytes 491528 | tf_op jit(solution)/shard_map/ppermute | solution.py:22
  5.3 6.1 %collective-permute-start.3 = (bf16[128,640]{1,0:T(8,128)(2,1)S(1)}, bf16[128,640]{1,0:T(8,128)(2,1)S(1)}, u32[]{:S(2)}, u32[]{:S(2)}) collective-permute-start(bf16[128,640]{1,0:T(8,128)(2,1)S(1)} %constant_dynamic-slice_fusion), channel_id=1, source_target_pairs={{0,96},{16,112},{32,0},{48,16},{64,32},{80,48},{96,64},{112,80},{1... | collective-permute-start | bytes 491528 | tf_op jit(solution)/shard_map/ppermute | solution.py:22
  7.5 6.7 %collective-permute-start.5 = (bf16[128,640]{1,0:T(8,128)(2,1)S(1)}, bf16[128,640]{1,0:T(8,128)(2,1)S(1)}, u32[]{:S(2)}, u32[]{:S(2)}) collective-permute-start(bf16[128,640]{1,0:T(8,128)(2,1)S(1)} %constant_dynamic-slice_fusion), channel_id=1, source_target_pairs={{0,16},{16,0},{32,48},{48,32},{64,80},{80,64},{96,112},{112,96},{1... | collective-permute-start | bytes 491528 | tf_op jit(solution)/shard_map/ppermute | solution.py:26
  11.3 17.0 %copy-start.23 = (bf16[128,640]{1,0:T(8,128)(2,1)}, bf16[128,640]{1,0:T(8,128)(2,1)S(1)}, u32[]{:S(2)}) copy-start(bf16[128,640]{1,0:T(8,128)(2,1)S(1)} %collective-permute-done.1.refs_1_) | copy-start | bytes 491524
  11.4 6.7 %collective-permute-start.11 = (bf16[64,640]{1,0:T(8,128)(2,1)S(1)}, bf16[64,640]{1,0:T(8,128)(2,1)S(1)}, u32[]{:S(2)}, u32[]{:S(2)}) collective-permute-start(bf16[64,640]{1,0:T(8,128)(2,1)S(1)} %slice.128), channel_id=1, source_target_pairs={{0,32},{16,48},{32,64},{48,80},{64,96},{80,112},{96,0},{112,16},{1... | collective-permute-start | bytes 245768 | tf_op jit(solution)/shard_map/ppermute | solution.py:22
  11.4 16.9 %copy-start.24 = (bf16[128,640]{1,0:T(8,128)(2,1)}, bf16[128,640]{1,0:T(8,128)(2,1)S(1)}, u32[]{:S(2)}) copy-start(bf16[128,640]{1,0:T(8,128)(2,1)S(1)} %collective-permute-done.3.refs_3_) | copy-start | bytes 491524
  11.5 6.8 %collective-permute-start.12 = (bf16[64,640]{1,0:T(8,128)(2,1)S(1)}, bf16[64,640]{1,0:T(8,128)(2,1)S(1)}, u32[]{:S(2)}, u32[]{:S(2)}) collective-permute-start(bf16[64,640]{1,0:T(8,128)(2,1)S(1)} %slice.129), channel_id=1, source_target_pairs={{0,96},{16,112},{32,0},{48,16},{64,32},{80,48},{96,64},{112,80},{1... | collective-permute-start | bytes 245768 | tf_op jit(solution)/shard_map/ppermute | solution.py:22
  14.2 14.2 %copy-start.28 = (bf16[128,640]{1,0:T(8,128)(2,1)}, bf16[128,640]{1,0:T(8,128)(2,1)S(1)}, u32[]{:S(2)}) copy-start(bf16[128,640]{1,0:T(8,128)(2,1)S(1)} %collective-permute-done.5.refs_5_) | copy-start | bytes 491524
  14.2 7.3 %collective-permute-start.9 = (bf16[128,640]{1,0:T(8,128)(2,1)S(1)}, bf16[128,640]{1,0:T(8,128)(2,1)S(1)}, u32[]{:S(2)}, u32[]{:S(2)}) collective-permute-start(bf16[128,640]{1,0:T(8,128)(2,1)S(1)} %collective-permute-done.5.refs_5_), channel_id=1, source_target_pairs={{0,96},{16,112},{32,0},{48,16},{64,32},{80,48},{96,64},{112,80},{1... | collective-permute-start | bytes 491528 | tf_op jit(solution)/shard_map/ppermute | solution.py:22
  14.6 7.5 %collective-permute-start.7 = (bf16[128,640]{1,0:T(8,128)(2,1)S(1)}, bf16[128,640]{1,0:T(8,128)(2,1)S(1)}, u32[]{:S(2)}, u32[]{:S(2)}) collective-permute-start(bf16[128,640]{1,0:T(8,128)(2,1)S(1)} %collective-permute-done.5.refs_5_), channel_id=1, source_target_pairs={{0,32},{16,48},{32,64},{48,80},{64,96},{80,112},{96,0},{112,16},{1... | collective-permute-start | bytes 491528 | tf_op jit(solution)/shard_map/ppermute | solution.py:22
  15.7 8.2 %collective-permute-start.6 = (bf16[128,640]{1,0:T(8,128)(2,1)S(1)}, bf16[128,640]{1,0:T(8,128)(2,1)S(1)}, u32[]{:S(2)}, u32[]{:S(2)}) collective-permute-start(bf16[128,640]{1,0:T(8,128)(2,1)S(1)} %collective-permute-done.5.refs_5_), channel_id=1, source_target_pairs={{0,1},{1,0},{2,3},{3,2},{4,5},{5,4},{6,7},{7,6},{8,9},{9,8},{10,11... | collective-permute-start | bytes 491528 | tf_op jit(solution)/shard_map/ppermute | solution.py:39
  18.0 5.9 %collective-permute-start.2 = (bf16[128,640]{1,0:T(8,128)(2,1)S(1)}, bf16[128,640]{1,0:T(8,128)(2,1)S(1)}, u32[]{:S(2)}, u32[]{:S(2)}) collective-permute-start(bf16[128,640]{1,0:T(8,128)(2,1)S(1)} %collective-permute-done.1.refs_1_), channel_id=1, source_target_pairs={{0,1},{1,0},{2,3},{3,2},{4,5},{5,4},{6,7},{7,6},{8,9},{9,8},{10,11... | collective-permute-start | bytes 491528 | tf_op jit(solution)/shard_map/ppermute | solution.py:39
  18.4 7.2 %collective-permute-start.14 = (bf16[128,640]{1,0:T(8,128)(2,1)S(1)}, bf16[128,640]{1,0:T(8,128)(2,1)}, u32[]{:S(2)}, u32[]{:S(2)}) collective-permute-start(bf16[128,640]{1,0:T(8,128)(2,1)S(1)} %constant_dynamic-update-slice_fusion.refs_11_), channel_id=1, source_target_pairs={{0,16},{16,0},{32,48},{48,32},{64,80},{80,64},{96,112},{112,96},{1... | collective-permute-start | bytes 491528 | tf_op jit(solution)/shard_map/ppermute | solution.py:26
  21.5 5.8 %collective-permute-start.4 = (bf16[128,640]{1,0:T(8,128)(2,1)S(1)}, bf16[128,640]{1,0:T(8,128)(2,1)S(1)}, u32[]{:S(2)}, u32[]{:S(2)}) collective-permute-start(bf16[128,640]{1,0:T(8,128)(2,1)S(1)} %collective-permute-done.3.refs_3_), channel_id=1, source_target_pairs={{0,1},{1,0},{2,3},{3,2},{4,5},{5,4},{6,7},{7,6},{8,9},{9,8},{10,11... | collective-permute-start | bytes 491528 | tf_op jit(solution)/shard_map/ppermute | solution.py:39
  22.1 5.5 %collective-permute-start.13 = (bf16[128,640]{1,0:T(8,128)(2,1)S(1)}, bf16[128,640]{1,0:T(8,128)(2,1)S(1)}, u32[]{:S(2)}, u32[]{:S(2)}) collective-permute-start(bf16[128,640]{1,0:T(8,128)(2,1)S(1)} %constant_dynamic-update-slice_fusion.refs_11_), channel_id=1, source_target_pairs={{0,1},{1,0},{2,3},{3,2},{4,5},{5,4},{6,7},{7,6},{8,9},{9,8},{10,11... | collective-permute-start | bytes 491528 | tf_op jit(solution)/shard_map/ppermute | solution.py:39
  23.8 3.8 %collective-permute-start.10 = (bf16[128,640]{1,0:T(8,128)(2,1)S(1)}, bf16[128,640]{1,0:T(8,128)(2,1)S(1)}, u32[]{:S(2)}, u32[]{:S(2)}) collective-permute-start(bf16[128,640]{1,0:T(8,128)(2,1)S(1)} %collective-permute-done.9.refs_9_), channel_id=1, source_target_pairs={{0,1},{1,0},{2,3},{3,2},{4,5},{5,4},{6,7},{7,6},{8,9},{9,8},{10,11... | collective-permute-start | bytes 491528 | tf_op jit(solution)/shard_map/ppermute | solution.py:39
  23.9 3.7 %collective-permute-start.8 = (bf16[128,640]{1,0:T(8,128)(2,1)S(1)}, bf16[128,640]{1,0:T(8,128)(2,1)S(1)}, u32[]{:S(2)}, u32[]{:S(2)}) collective-permute-start(bf16[128,640]{1,0:T(8,128)(2,1)S(1)} %collective-permute-done.7.refs_7_), channel_id=1, source_target_pairs={{0,1},{1,0},{2,3},{3,2},{4,5},{5,4},{6,7},{7,6},{8,9},{9,8},{10,11... | collective-permute-start | bytes 491528 | tf_op jit(solution)/shard_map/ppermute | solution.py:39
  25.6 2.8 %collective-permute-start.15 = (bf16[128,640]{1,0:T(8,128)(2,1)}, bf16[128,640]{1,0:T(8,128)(2,1)}, u32[]{:S(2)}, u32[]{:S(2)}) collective-permute-start(bf16[128,640]{1,0:T(8,128)(2,1)} %collective-permute-done.14.refs_13_), channel_id=1, source_target_pairs={{0,1},{1,0},{2,3},{3,2},{4,5},{5,4},{6,7},{7,6},{8,9},{9,8},{10,11... | collective-permute-start | bytes 491528 | tf_op jit(solution)/shard_map/ppermute | solution.py:39
  27.3 49.2 %collective-permute-start = (bf16[1024,896]{1,0:T(8,128)(2,1)S(1)}, bf16[1024,896]{1,0:T(8,128)(2,1)}, u32[]{:S(2)}, u32[]{:S(2)}) collective-permute-start(bf16[1024,896]{1,0:T(8,128)(2,1)S(1)} %copy-done.2), channel_id=1, source_target_pairs={{0,1},{1,0},{2,3},{3,2},{4,5},{5,4},{6,7},{7,6},{8,9},{9,8},{10,11... | collective-permute-start | bytes 5505032 | tf_op jit(solution)/shard_map/ppermute | solution.py:39
  48.0 28.1 %copy-start.26 = (s32[128,4]{0,1:T(4,128)S(1)}, s32[128,4]{0,1:T(4,128)}, u32[]{:S(2)}) copy-start(s32[128,4]{0,1:T(4,128)} %param.22) | copy-start | bytes 6148
  48.0 1.9 collective-permute-start.16
  50.0 14.5 %collective-permute-start.20 = (bf16[128,2048]{1,0:T(8,128)(2,1)S(1)}, bf16[128,2048]{1,0:T(8,128)(2,1)S(1)}, u32[]{:S(2)}, u32[]{:S(2)}) collective-permute-start(bf16[128,2048]{1,0:T(8,128)(2,1)S(1)} %constant_dynamic-update-slice_fusion.2.refs_2_), channel_id=1, source_target_pairs={{0,32},{16,48},{32,64},{48,80},{64,96},{80,112},{96,0},{112,16},{1... | collective-permute-start | bytes 1572872 | tf_op jit(solution)/shard_map/ppermute | solution.py:22
  50.0 14.6 %collective-permute-start.23 = (bf16[128,2048]{1,0:T(8,128)(2,1)S(1)}, bf16[128,2048]{1,0:T(8,128)(2,1)S(1)}, u32[]{:S(2)}, u32[]{:S(2)}) collective-permute-start(bf16[128,2048]{1,0:T(8,128)(2,1)S(1)} %constant_dynamic-update-slice_fusion.2.refs_2_), channel_id=1, source_target_pairs={{0,96},{16,112},{32,0},{48,16},{64,32},{80,48},{96,64},{112,80},{1... | collective-permute-start | bytes 1572872 | tf_op jit(solution)/shard_map/ppermute | solution.py:22
  52.7 14.6 %collective-permute-start.17 = (bf16[128,2048]{1,0:T(8,128)(2,1)S(1)}, bf16[128,2048]{1,0:T(8,128)(2,1)}, u32[]{:S(2)}, u32[]{:S(2)}) collective-permute-start(bf16[128,2048]{1,0:T(8,128)(2,1)S(1)} %constant_dynamic-update-slice_fusion.2.refs_2_), channel_id=1, source_target_pairs={{0,16},{16,0},{32,48},{48,32},{64,80},{80,64},{96,112},{112,96},{1... | collective-permute-start | bytes 1572872 | tf_op jit(solution)/shard_map/ppermute | solution.py:26
  64.5 10.8 %copy-start.4 = (bf16[128,2048]{1,0:T(8,128)(2,1)}, bf16[128,2048]{1,0:T(8,128)(2,1)S(1)}, u32[]{:S(2)}) copy-start(bf16[128,2048]{1,0:T(8,128)(2,1)S(1)} %collective-permute-done.20.refs_3_) | copy-start | bytes 1572868
  64.5 8.1 %collective-permute-start.21 = (bf16[64,2048]{1,0:T(8,128)(2,1)S(1)}, bf16[64,2048]{1,0:T(8,128)(2,1)}, u32[]{:S(2)}, u32[]{:S(2)}) collective-permute-start(bf16[64,2048]{1,0:T(8,128)(2,1)S(1)} %slice.130), channel_id=1, source_target_pairs={{0,32},{16,48},{32,64},{48,80},{64,96},{80,112},{96,0},{112,16},{1... | collective-permute-start | bytes 786440 | tf_op jit(solution)/shard_map/ppermute | solution.py:22
  64.6 10.7 %copy-start.6 = (bf16[128,2048]{1,0:T(8,128)(2,1)}, bf16[128,2048]{1,0:T(8,128)(2,1)S(1)}, u32[]{:S(2)}) copy-start(bf16[128,2048]{1,0:T(8,128)(2,1)S(1)} %collective-permute-done.23.refs_4_) | copy-start | bytes 1572868
  64.6 10.6 %collective-permute-start.24 = (bf16[64,2048]{1,0:T(8,128)(2,1)S(1)}, bf16[64,2048]{1,0:T(8,128)(2,1)}, u32[]{:S(2)}, u32[]{:S(2)}) collective-permute-start(bf16[64,2048]{1,0:T(8,128)(2,1)S(1)} %slice.131), channel_id=1, source_target_pairs={{0,96},{16,112},{32,0},{48,16},{64,32},{80,48},{96,64},{112,80},{1... | collective-permute-start | bytes 786440 | tf_op jit(solution)/shard_map/ppermute | solution.py:22
  67.4 17.8 %collective-permute-start.18 = (bf16[128,2048]{1,0:T(8,128)(2,1)}, bf16[128,2048]{1,0:T(8,128)(2,1)S(1)}, u32[]{:S(2)}, u32[]{:S(2)}) collective-permute-start(bf16[128,2048]{1,0:T(8,128)(2,1)} %collective-permute-done.17.refs_5_), channel_id=1, source_target_pairs={{0,32},{16,48},{32,64},{48,80},{64,96},{80,112},{96,0},{112,16},{1... | collective-permute-start | bytes 1572872 | tf_op jit(solution)/shard_map/ppermute | solution.py:22
  67.4 17.8 %collective-permute-start.19 = (bf16[128,2048]{1,0:T(8,128)(2,1)}, bf16[128,2048]{1,0:T(8,128)(2,1)S(1)}, u32[]{:S(2)}, u32[]{:S(2)}) collective-permute-start(bf16[128,2048]{1,0:T(8,128)(2,1)} %collective-permute-done.17.refs_5_), channel_id=1, source_target_pairs={{0,96},{16,112},{32,0},{48,16},{64,32},{80,48},{96,64},{112,80},{1... | collective-permute-start | bytes 1572872 | tf_op jit(solution)/shard_map/ppermute | solution.py:22
  72.6 12.5 %collective-permute-start.22 = (bf16[64,2048]{1,0:T(8,128)(2,1)}, bf16[64,2048]{1,0:T(8,128)(2,1)S(1)}, u32[]{:S(2)}, u32[]{:S(2)}) collective-permute-start(bf16[64,2048]{1,0:T(8,128)(2,1)} %collective-permute-done.21.refs_6_), channel_id=1, source_target_pairs={{0,16},{16,0},{32,48},{48,32},{64,80},{80,64},{96,112},{112,96},{1... | collective-permute-start | bytes 786440 | tf_op jit(solution)/shard_map/ppermute | solution.py:26
  75.3 9.8 %collective-permute-start.25 = (bf16[64,2048]{1,0:T(8,128)(2,1)}, bf16[64,2048]{1,0:T(8,128)(2,1)S(1)}, u32[]{:S(2)}, u32[]{:S(2)}) collective-permute-start(bf16[64,2048]{1,0:T(8,128)(2,1)} %collective-permute-done.24.refs_7_), channel_id=1, source_target_pairs={{0,16},{16,0},{32,48},{48,32},{64,80},{80,64},{96,112},{112,96},{1... | collective-permute-start | bytes 786440 | tf_op jit(solution)/shard_map/ppermute | solution.py:26
  89.2 6.2 %collective-permute-start.26 = (bf16[128,896]{1,0:T(8,128)(2,1)S(1)}, bf16[128,896]{1,0:T(8,128)(2,1)S(1)}, u32[]{:S(2)}, u32[]{:S(2)}) collective-permute-start(bf16[128,896]{1,0:T(8,128)(2,1)S(1)} %get-tuple-element.24), channel_id=1, source_target_pairs={{0,4},{1,5},{2,6},{3,7},{4,8},{5,9},{6,10},{7,11},{8,12},{9,13},{1... | collective-permute-start | bytes 688136 | tf_op jit(solution)/shard_map/ppermute | solution.py:31
  90.5 4.9 %collective-permute-start.27 = (bf16[128,896]{1,0:T(8,128)(2,1)S(1)}, bf16[128,896]{1,0:T(8,128)(2,1)S(1)}, u32[]{:S(2)}, u32[]{:S(2)}) collective-permute-start(bf16[128,896]{1,0:T(8,128)(2,1)S(1)} %get-tuple-element.26), channel_id=1, source_target_pairs={{0,12},{1,13},{2,14},{3,15},{4,0},{5,1},{6,2},{7,3},{8,4},{9,5},{1... | collective-permute-start | bytes 688136 | tf_op jit(solution)/shard_map/ppermute | solution.py:31
  92.0 4.9 %collective-permute-start.29 = (bf16[128,896]{1,0:T(8,128)(2,1)S(1)}, bf16[128,896]{1,0:T(8,128)(2,1)S(1)}, u32[]{:S(2)}, u32[]{:S(2)}) collective-permute-start(bf16[128,896]{1,0:T(8,128)(2,1)S(1)} %get-tuple-element.25), channel_id=1, source_target_pairs={{0,2},{1,3},{2,0},{3,1},{4,6},{5,7},{6,4},{7,5},{8,10},{9,11},{10,... | collective-permute-start | bytes 688136 | tf_op jit(solution)/shard_map/ppermute | solution.py:35
  97.0 4.9 %collective-permute-start.30 = (bf16[64,896]{1,0:T(8,128)(2,1)S(1)}, bf16[64,896]{1,0:T(8,128)(2,1)S(1)}, u32[]{:S(2)}, u32[]{:S(2)}) collective-permute-start(bf16[64,896]{1,0:T(8,128)(2,1)S(1)} %get-tuple-element.33), channel_id=1, source_target_pairs={{0,4},{1,5},{2,6},{3,7},{4,8},{5,9},{6,10},{7,11},{8,12},{9,13},{1... | collective-permute-start | bytes 344072 | tf_op jit(solution)/shard_map/ppermute | solution.py:31
  97.1 4.8 %collective-permute-start.32 = (bf16[64,896]{1,0:T(8,128)(2,1)S(1)}, bf16[64,896]{1,0:T(8,128)(2,1)S(1)}, u32[]{:S(2)}, u32[]{:S(2)}) collective-permute-start(bf16[64,896]{1,0:T(8,128)(2,1)S(1)} %get-tuple-element.34), channel_id=1, source_target_pairs={{0,12},{1,13},{2,14},{3,15},{4,0},{5,1},{6,2},{7,3},{8,4},{9,5},{1... | collective-permute-start | bytes 344072 | tf_op jit(solution)/shard_map/ppermute | solution.py:31
  99.8 5.4 %collective-permute-start.28 = (bf16[128,896]{1,0:T(8,128)(2,1)S(1)}, bf16[128,896]{1,0:T(8,128)(2,1)S(1)}, u32[]{:S(2)}, u32[]{:S(2)}) collective-permute-start(bf16[128,896]{1,0:T(8,128)(2,1)S(1)} %get-tuple-element.22), channel_id=1, source_target_pairs={{0,2},{1,3},{2,0},{3,1},{4,6},{5,7},{6,4},{7,5},{8,10},{9,11},{10,... | collective-permute-start | bytes 688136 | tf_op jit(solution)/shard_map/ppermute | solution.py:35
  102.1 7.6 %collective-permute-start.31 = (bf16[128,896]{1,0:T(8,128)(2,1)S(1)}, bf16[128,896]{1,0:T(8,128)(2,1)S(1)}, u32[]{:S(2)}, u32[]{:S(2)}) collective-permute-start(bf16[128,896]{1,0:T(8,128)(2,1)S(1)} %pad_maximum_fusion.3), channel_id=1, source_target_pairs={{0,4},{1,5},{2,6},{3,7},{4,8},{5,9},{6,10},{7,11},{8,12},{9,13},{1... | collective-permute-start | bytes 688136 | tf_op jit(solution)/shard_map/ppermute | solution.py:31
  103.2 6.5 %collective-permute-start.33 = (bf16[128,896]{1,0:T(8,128)(2,1)S(1)}, bf16[128,896]{1,0:T(8,128)(2,1)S(1)}, u32[]{:S(2)}, u32[]{:S(2)}) collective-permute-start(bf16[128,896]{1,0:T(8,128)(2,1)S(1)} %pad_maximum_fusion.4), channel_id=1, source_target_pairs={{0,12},{1,13},{2,14},{3,15},{4,0},{5,1},{6,2},{7,3},{8,4},{9,5},{1... | collective-permute-start | bytes 688136 | tf_op jit(solution)/shard_map/ppermute | solution.py:31
  111.5 32.5 %all-to-all-start = ((bf16[16,48,896]{2,1,0:T(8,128)(2,1)}), bf16[16,48,896]{2,1,0:T(8,128)(2,1)S(1)}, u32[]{:S(2)}, u32[]{:S(2)}) async-start(bf16[16,48,896]{2,1,0:T(8,128)(2,1)} %bitcast.39), calls=%async_computation | async-start | bytes 2752512 | tf_op jit(solution)/shard_map/all_to_all | solution.py:350
  146.0 19.8 %collective-permute-start.37 = (bf16[768,512]{1,0:T(8,128)(2,1)S(1)}, bf16[768,512]{1,0:T(8,128)(2,1)S(1)}, u32[]{:S(2)}, u32[]{:S(2)}) collective-permute-start(bf16[768,512]{1,0:T(8,128)(2,1)S(1)} %convolution_convert_fusion.2), channel_id=1, source_target_pairs={{0,16},{16,0},{32,48},{48,32},{64,80},{80,64},{96,112},{112,96},{1... | collective-permute-start | bytes 2359304 | tf_op jit(solution)/shard_map/ppermute | solution.py:26
  149.8 21.0 %collective-permute-start.34 = (bf16[768,512]{1,0:T(8,128)(2,1)S(1)}, bf16[768,512]{1,0:T(8,128)(2,1)S(1)}, u32[]{:S(2)}, u32[]{:S(2)}) collective-permute-start(bf16[768,512]{1,0:T(8,128)(2,1)S(1)} %convolution_convert_fusion.6), channel_id=1, source_target_pairs={{0,32},{16,48},{32,64},{48,80},{64,96},{80,112},{96,0},{112,16},{1... | collective-permute-start | bytes 2359304 | tf_op jit(solution)/shard_map/ppermute | solution.py:22
  151.0 19.8 %collective-permute-start.35 = (bf16[768,512]{1,0:T(8,128)(2,1)S(1)}, bf16[768,512]{1,0:T(8,128)(2,1)S(1)}, u32[]{:S(2)}, u32[]{:S(2)}) collective-permute-start(bf16[768,512]{1,0:T(8,128)(2,1)S(1)} %convolution_convert_fusion.5), channel_id=1, source_target_pairs={{0,96},{16,112},{32,0},{48,16},{64,32},{80,48},{96,64},{112,80},{1... | collective-permute-start | bytes 2359304 | tf_op jit(solution)/shard_map/ppermute | solution.py:22
  153.9 11.9 %copy-start.16 = (bf16[896,256]{1,0:T(8,128)(2,1)S(1)}, bf16[896,256]{1,0:T(8,128)(2,1)}, u32[]{:S(2)}) copy-start(bf16[896,256]{1,0:T(8,128)(2,1)} %get-tuple-element.15) | copy-start | bytes 1376260
  153.9 11.9 %copy-start.17 = (bf16[896,256]{1,0:T(8,128)(2,1)S(1)}, bf16[896,256]{1,0:T(8,128)(2,1)}, u32[]{:S(2)}) copy-start(bf16[896,256]{1,0:T(8,128)(2,1)} %get-tuple-element.41) | copy-start | bytes 1376260
  166.9 10.1 %collective-permute-start.38 = (bf16[384,512]{1,0:T(8,128)(2,1)S(1)}, bf16[384,512]{1,0:T(8,128)(2,1)S(1)}, u32[]{:S(2)}, u32[]{:S(2)}) collective-permute-start(bf16[384,512]{1,0:T(8,128)(2,1)S(1)} %get-tuple-element.31), channel_id=1, source_target_pairs={{0,32},{16,48},{32,64},{48,80},{64,96},{80,112},{96,0},{112,16},{1... | collective-permute-start | bytes 1179656 | tf_op jit(solution)/shard_map/ppermute | solution.py:22
  169.0 8.9 %collective-permute-start.40 = (bf16[384,512]{1,0:T(8,128)(2,1)S(1)}, bf16[384,512]{1,0:T(8,128)(2,1)S(1)}, u32[]{:S(2)}, u32[]{:S(2)}) collective-permute-start(bf16[384,512]{1,0:T(8,128)(2,1)S(1)} %get-tuple-element.32), channel_id=1, source_target_pairs={{0,96},{16,112},{32,0},{48,16},{64,32},{80,48},{96,64},{112,80},{1... | collective-permute-start | bytes 1179656 | tf_op jit(solution)/shard_map/ppermute | solution.py:22
  171.8 18.3 %collective-permute-start.36 = (bf16[768,512]{1,0:T(8,128)(2,1)S(1)}, bf16[768,512]{1,0:T(8,128)(2,1)S(1)}, u32[]{:S(2)}, u32[]{:S(2)}) collective-permute-start(bf16[768,512]{1,0:T(8,128)(2,1)S(1)} %add_convert_fusion.1), channel_id=1, source_target_pairs={{0,16},{16,0},{32,48},{48,32},{64,80},{80,64},{96,112},{112,96},{1... | collective-permute-start | bytes 2359304 | tf_op jit(solution)/shard_map/ppermute | solution.py:26
  177.2 17.6 %collective-permute-start.39 = (bf16[768,512]{1,0:T(8,128)(2,1)S(1)}, bf16[768,512]{1,0:T(8,128)(2,1)S(1)}, u32[]{:S(2)}, u32[]{:S(2)}) collective-permute-start(bf16[768,512]{1,0:T(8,128)(2,1)S(1)} %pad_maximum_fusion), channel_id=1, source_target_pairs={{0,32},{16,48},{32,64},{48,80},{64,96},{80,112},{96,0},{112,16},{1... | collective-permute-start | bytes 2359304 | tf_op jit(solution)/shard_map/ppermute | solution.py:22
  178.1 16.7 %collective-permute-start.41 = (bf16[768,512]{1,0:T(8,128)(2,1)S(1)}, bf16[768,512]{1,0:T(8,128)(2,1)S(1)}, u32[]{:S(2)}, u32[]{:S(2)}) collective-permute-start(bf16[768,512]{1,0:T(8,128)(2,1)S(1)} %pad_maximum_fusion.1), channel_id=1, source_target_pairs={{0,96},{16,112},{32,0},{48,16},{64,32},{80,48},{96,64},{112,80},{1... | collective-permute-start | bytes 2359304 | tf_op jit(solution)/shard_map/ppermute | solution.py:22
  195.4 9.0 %collective-permute-start.45 = (bf16[768,256]{1,0:T(8,128)(2,1)S(1)}, bf16[768,256]{1,0:T(8,128)(2,1)S(1)}, u32[]{:S(2)}, u32[]{:S(2)}) collective-permute-start(bf16[768,256]{1,0:T(8,128)(2,1)S(1)} %fusion.26.refs_0_), channel_id=1, source_target_pairs={{0,32},{16,48},{32,64},{48,80},{64,96},{80,112},{96,0},{112,16},{1... | collective-permute-start | bytes 1179656 | tf_op jit(solution)/shard_map/ppermute | solution.py:22
  195.5 9.0 %collective-permute-start.48 = (bf16[768,256]{1,0:T(8,128)(2,1)S(1)}, bf16[768,256]{1,0:T(8,128)(2,1)S(1)}, u32[]{:S(2)}, u32[]{:S(2)}) collective-permute-start(bf16[768,256]{1,0:T(8,128)(2,1)S(1)} %fusion.26.refs_0_), channel_id=1, source_target_pairs={{0,96},{16,112},{32,0},{48,16},{64,32},{80,48},{96,64},{112,80},{1... | collective-permute-start | bytes 1179656 | tf_op jit(solution)/shard_map/ppermute | solution.py:22
  198.9 8.3 %collective-permute-start.42 = (bf16[768,256]{1,0:T(8,128)(2,1)S(1)}, bf16[768,256]{1,0:T(8,128)(2,1)S(1)}, u32[]{:S(2)}, u32[]{:S(2)}) collective-permute-start(bf16[768,256]{1,0:T(8,128)(2,1)S(1)} %fusion.26.refs_0_), channel_id=1, source_target_pairs={{0,16},{16,0},{32,48},{48,32},{64,80},{80,64},{96,112},{112,96},{1... | collective-permute-start | bytes 1179656 | tf_op jit(solution)/shard_map/ppermute | solution.py:26
  204.4 6.2 %collective-permute-start.46 = (bf16[384,256]{1,0:T(8,128)(2,1)S(1)}, bf16[384,256]{1,0:T(8,128)(2,1)S(1)}, u32[]{:S(2)}, u32[]{:S(2)}) collective-permute-start(bf16[384,256]{1,0:T(8,128)(2,1)S(1)} %slice.153), channel_id=1, source_target_pairs={{0,32},{16,48},{32,64},{48,80},{64,96},{80,112},{96,0},{112,16},{1... | collective-permute-start | bytes 589832 | tf_op jit(solution)/shard_map/ppermute | solution.py:22
  204.6 8.5 %collective-permute-start.49 = (bf16[384,256]{1,0:T(8,128)(2,1)S(1)}, bf16[384,256]{1,0:T(8,128)(2,1)S(1)}, u32[]{:S(2)}, u32[]{:S(2)}) collective-permute-start(bf16[384,256]{1,0:T(8,128)(2,1)S(1)} %slice.154), channel_id=1, source_target_pairs={{0,96},{16,112},{32,0},{48,16},{64,32},{80,48},{96,64},{112,80},{1... | collective-permute-start | bytes 589832 | tf_op jit(solution)/shard_map/ppermute | solution.py:22
  207.3 12.9 %collective-permute-start.43 = (bf16[768,256]{1,0:T(8,128)(2,1)S(1)}, bf16[768,256]{1,0:T(8,128)(2,1)S(1)}, u32[]{:S(2)}, u32[]{:S(2)}) collective-permute-start(bf16[768,256]{1,0:T(8,128)(2,1)S(1)} %collective-permute-done.42.refs_3_), channel_id=1, source_target_pairs={{0,32},{16,48},{32,64},{48,80},{64,96},{80,112},{96,0},{112,16},{1... | collective-permute-start | bytes 1179656 | tf_op jit(solution)/shard_map/ppermute | solution.py:22
  207.3 12.9 %collective-permute-start.44 = (bf16[768,256]{1,0:T(8,128)(2,1)S(1)}, bf16[768,256]{1,0:T(8,128)(2,1)S(1)}, u32[]{:S(2)}, u32[]{:S(2)}) collective-permute-start(bf16[768,256]{1,0:T(8,128)(2,1)S(1)} %collective-permute-done.42.refs_3_), channel_id=1, source_target_pairs={{0,96},{16,112},{32,0},{48,16},{64,32},{80,48},{96,64},{112,80},{1... | collective-permute-start | bytes 1179656 | tf_op jit(solution)/shard_map/ppermute | solution.py:22
  210.6 9.5 %collective-permute-start.47 = (bf16[384,256]{1,0:T(8,128)(2,1)S(1)}, bf16[384,256]{1,0:T(8,128)(2,1)S(1)}, u32[]{:S(2)}, u32[]{:S(2)}) collective-permute-start(bf16[384,256]{1,0:T(8,128)(2,1)S(1)} %collective-permute-done.46.refs_4_), channel_id=1, source_target_pairs={{0,16},{16,0},{32,48},{48,32},{64,80},{80,64},{96,112},{112,96},{1... | collective-permute-start | bytes 589832 | tf_op jit(solution)/shard_map/ppermute | solution.py:26
  213.1 7.1 %collective-permute-start.50 = (bf16[384,256]{1,0:T(8,128)(2,1)S(1)}, bf16[384,256]{1,0:T(8,128)(2,1)S(1)}, u32[]{:S(2)}, u32[]{:S(2)}) collective-permute-start(bf16[384,256]{1,0:T(8,128)(2,1)S(1)} %collective-permute-done.49.refs_5_), channel_id=1, source_target_pairs={{0,16},{16,0},{32,48},{48,32},{64,80},{80,64},{96,112},{112,96},{1... | collective-permute-start | bytes 589832 | tf_op jit(solution)/shard_map/ppermute | solution.py:26
  224.2 14.6 %copy-start.27 = (bf16[128,4]{0,1:T(4,128)(2,1)S(1)}, bf16[128,4]{0,1:T(4,128)(2,1)}, u32[]{:S(2)}) copy-start(bf16[128,4]{0,1:T(4,128)(2,1)} %param.23) | copy-start | bytes 3076
  224.3 33.8 %all-to-all-start.1 = ((bf16[16,48,896]{2,1,0:T(8,128)(2,1)}), bf16[16,48,896]{2,1,0:T(8,128)(2,1)S(1)}, u32[]{:S(2)}, u32[]{:S(2)}) async-start(bf16[16,48,896]{2,1,0:T(8,128)(2,1)} %bitcast.62), calls=%async_computation.1 | async-start | bytes 2752512 | tf_op jit(solution)/shard_map/all_to_all | solution.py:368
  (26 other events, 82.4 us)
